TPU v7x, 256 devices: a whole 4x4x8 slice. The times are simulated.
256 devices in a mesh: lat: 16 (over z_hi, x), lev: 16 (over z_lo, y, core).
Axes of the slice: x: 4, y: 4, z: 8 (z_hi: 4, z_lo: 2; z = z_hi * 2 + z_lo), core: 2. Of those that a mesh axis runs over, the one named last changes fastest.
Arguments:
- tracer: float32 [32, 256, 2304], P('lev', 'lat'), may hold values from 0.5 to 2
- thickness: float32 [32, 256, 2304], P('lev', 'lat'), may hold values from 0.5 to 1.5
- wind_u: float32 [32, 256, 2304], P('lev', 'lat'), may hold values from -4 to 4
- wind_v: float32 [32, 256, 2304], P('lev', 'lat'), may hold values from -4 to 4
- offsets: int32 [32, 256, 2304], P(None, 'lat', 'lev'), may hold values from 0 to 2
- coupling: float32 [31, 256, 2304], P(None, 'lat', 'lev'), may hold values from 0.1 to 10
Outputs:
- tracer_out: float32 [32, 256, 2304], P('lev', 'lat')
- wind_u_out: float32 [32, 256, 2304], P('lev', 'lat')
- wind_v_out: float32 [32, 256, 2304], P('lev', 'lat')
All inputs are finite; a program needn't handle non-finite values.
Results may differ from a plain program's by a relative error of at most 0.00002.
Values sent between devices are 32-bit elements; how exact they have to be, the bound alone decides.
No kernel may reach another device: no remote copies, remote signals or barrier semaphores. Data moves between devices by JAX's collectives and lax.ppermute only.
A program may use at most 64 MiB of HBM per device.

v0:
```python
import jax
import jax.numpy as jnp
from jax import lax
from jax.experimental import pallas as pl
from jax.experimental.pallas import tpu as pltpu
from jax.sharding import PartitionSpec as P

courant_max = 0.24
LEVELS = 32
LON = 2304
ROWS = 16
DEST = 16
COLS = 144
LANES = 128
VM = pl.BlockSpec(memory_space=pltpu.VMEM)
SM = pl.BlockSpec(memory_space=pltpu.SMEM)
PARAMS = pltpu.CompilerParams(vmem_limit_bytes=24 * 1024 * 1024)


def lane_ids(rows):
    return lax.broadcasted_iota(jnp.int32, (rows, LANES), 1)


def row_ids(rows):
    return lax.broadcasted_iota(jnp.int32, (rows, LON), 0)


def courant(pair_sum):
    return courant_max * jnp.tanh(0.5 * pair_sum)


def upwind(flow, before, after):
    return jnp.maximum(flow, 0.0) * before + jnp.minimum(flow, 0.0) * after


def east_roll(x):
    return pltpu.roll(x, 1, 1)


def west_roll(x):
    return pltpu.roll(x, LON - 1, 1)


def zonal(east, mass):
    flux = upwind(east, east_roll(mass), mass)
    return flux - west_roll(flux)


def edge_kernel(tracer, thickness, wind_u, wind_v, to_north, to_south):
    def edges(ref):
        return jnp.concatenate(
            [ref[0, 0:2], ref[0, 14:16], ref[1, 0:2], ref[1, 14:16]], axis=0
        )

    u, v, layer = edges(wind_u), edges(wind_v), edges(thickness)
    mass = edges(tracer) * layer
    east = courant(east_roll(u) + u)
    north = courant(v + pltpu.roll(v, 7, 0))
    odd = lax.rem(row_ids(8), 2) == 1

    def partial(m):
        flux = upwind(north, m, pltpu.roll(m, 7, 0))
        return m + zonal(east, m) + jnp.where(odd, pltpu.roll(flux, 1, 0), -flux)

    for slot, value in enumerate((v, layer, mass, partial(layer), partial(mass))):
        for level in range(2):
            to_south[slot, level : level + 1, :] = value[4 * level : 4 * level + 1]
            to_north[slot, level : level + 1, :] = value[4 * level + 3 : 4 * level + 4]


def first_kernel(tracer, thickness, wind_u, wind_v, east_out, north_out, layer_out, mass_out):
    row = row_ids(ROWS)
    for level in range(2):
        u, v, layer = wind_u[level], wind_v[level], thickness[level]
        mass = tracer[level] * layer
        east = courant(east_roll(u) + u)
        north = jnp.where(row == 0, 0.0, courant(pltpu.roll(v, 1, 0) + v))
        east_out[level] = east
        north_out[level] = north
        for m, out in ((layer, layer_out), (mass, mass_out)):
            flux = upwind(north, pltpu.roll(m, 1, 0), m)
            above = jnp.where(row == ROWS - 1, 0.0, pltpu.roll(flux, ROWS - 1, 0))
            out[level] = m + zonal(east, m) + flux - above


def second_kernel(
    inside, tracer, thickness, wind_u, wind_v, east_in, north_in, layer_in, mass_in, south, north_halo, send, held
):
    row = row_ids(ROWS)
    first, last = row == 0, row == ROWS - 1
    for level in range(2):
        east = east_in[level]

        def south_row(slot):
            return south[slot, level : level + 1, :]

        def north_row(slot):
            return north_halo[slot, level : level + 1, :]

        v_low, v_high = wind_v[level, 0:1], wind_v[level, ROWS - 1 : ROWS]
        flow_low = inside[0] * courant(south_row(0) + v_low)
        flow_high = inside[1] * courant(v_high + north_row(0))
        north = jnp.where(first, flow_low, north_in[level])
        layer_low, layer_high = thickness[level, 0:1], thickness[level, ROWS - 1 : ROWS]
        mass_low = tracer[level, 0:1] * layer_low
        mass_high = tracer[level, ROWS - 1 : ROWS] * layer_high
        done = []
        for slot, low, high, partial in (
            (1, layer_low, layer_high, layer_in),
            (2, mass_low, mass_high, mass_in),
        ):
            flux_low = upwind(flow_low, south_row(slot), low)
            flux_high = upwind(flow_high, high, north_row(slot))
            m = partial[level] + jnp.where(first, flux_low, 0.0) - jnp.where(last, flux_high, 0.0)
            m_south = south_row(slot + 2) - flux_low
            m_north = north_row(slot + 2) + flux_high
            flux = upwind(north, jnp.where(first, m_south, pltpu.roll(m, 1, 0)), m)
            top = upwind(flow_high, m[ROWS - 1 : ROWS], m_north)
            above = jnp.where(last, top, pltpu.roll(flux, ROWS - 1, 0))
            done.append(m + zonal(east, m) + flux - above)
        layer, mass = done
        held[0, level] = mass
        held[1, level] = layer * wind_u[level]
        held[2, level] = layer * wind_v[level]
        held[3, level] = layer
    lane = lane_ids(ROWS)
    lane8 = lane_ids(8)
    for dest in range(DEST):
        tile = dest + dest // 8
        shift = 16 * (dest % 8)
        low = slice(tile * LANES, (tile + 1) * LANES)
        high = slice((tile + 1) * LANES, (tile + 2) * LANES)
        for level in range(2):
            packed = None
            for field in range(4):
                here = held[field, level, :, low]
                after = held[field, level, :, high]
                block = here if shift == 0 else jnp.where(lane >= shift, here, after)
                start = (field * 2 + level) * ROWS
                send[dest, start : start + ROWS, :] = block
                for half in range(2):
                    place = 32 * field + 16 * half
                    part = pltpu.roll(after[8 * half : 8 * half + 8], (place - shift) % LANES, 1)
                    packed = part if packed is None else jnp.where(lane8 >= place, part, packed)
            send[dest, 128 + 8 * level : 136 + 8 * level, :] = packed


def factor_kernel(shift_ref, offsets, coupling, choose_main, choose_rest, factors_main, factors_rest):
    shift = shift_ref[0]

    def main(ref, k):
        return pltpu.roll(ref[k, :, 0:LANES], shift, 1)

    def rest(ref, k):
        part = ref[k, :, LANES:COLS]
        both = jnp.concatenate([part[0:8], part[8:16]], axis=1)
        return jnp.concatenate([both, both, both, both], axis=1)

    for load, choose, factors, shape in (
        (main, choose_main, factors_main, (ROWS, LANES)),
        (rest, choose_rest, factors_rest, (8, LANES)),
    ):
        low = jnp.zeros(shape, jnp.float32)
        back = jnp.zeros(shape, jnp.float32)
        for k in range(LEVELS):
            choose[k] = load(offsets, k)
            high = load(coupling, k) if k < LEVELS - 1 else jnp.zeros(shape, jnp.float32)
            scale = 1.0 / (1.0 + low + high - low * back)
            back = high * scale
            factors[0, k] = scale
            factors[1, k] = low * scale
            factors[2, k] = back
            low = high


def column_kernel(received, choose_main, choose_rest, factors_main, factors_rest, send):
    lane = lane_ids(8)

    def main(k):
        base = (k % 2) * ROWS
        return [received[k // 2, base + 32 * f : base + 32 * f + ROWS, :] for f in range(4)]

    def rest(k):
        base = 128 + 8 * (k % 2)
        return received[k // 2, base : base + 8, :]

    def picked(choose, sums):
        return jnp.where(choose == 0, sums[0], jnp.where(choose == 1, sums[1], sums[2]))

    solve_main = [jnp.zeros((ROWS, LANES), jnp.float32)] * 3
    solve_rest = jnp.zeros((8, LANES), jnp.float32)
    main_here, rest_here = main(0), rest(0)
    main_sums, rest_sums = [], []

    def push(k):
        nonlocal main_here, rest_here
        main_next, rest_next = main(k + 1), rest(k + 1)
        main_sums.append([a + b for a, b in zip(main_here, main_next)])
        rest_sums.append(rest_here + rest_next)
        main_here, rest_here = main_next, rest_next

    push(0)
    for k in range(LEVELS):
        if k + 1 < LEVELS - 1:
            push(k + 1)
        three = [max(k - 1, 0), min(k, LEVELS - 2), min(k + 1, LEVELS - 2)]
        choose = choose_main[k]
        values = [picked(choose, [main_sums[i][f] for i in three]) for f in range(4)]
        weight = factors_main[0, k] / values[3]
        low = factors_main[1, k]
        solve_main = [values[f] * weight + low * solve_main[f] for f in range(3)]
        for f in range(3):
            base = (f * 2 + k % 2) * ROWS
            send[k // 2, base : base + ROWS, :] = solve_main[f]
        value = picked(choose_rest[k], [rest_sums[i] for i in three])
        total = jnp.where(lane >= 64, pltpu.roll(value, 96, 1), pltpu.roll(value, 32, 1))
        total = jnp.where(lane >= 32, jnp.where(lane >= 64, total, pltpu.roll(value, 64, 1)), total)
        solve_rest = value * (factors_rest[0, k] / total) + factors_rest[1, k] * solve_rest
        base = 96 + 8 * (k % 2)
        send[k // 2, base : base + 8, :] = solve_rest
    for k in range(LEVELS - 2, -1, -1):
        back = factors_main[2, k]
        for f in range(3):
            base = (f * 2 + k % 2) * ROWS
            solve_main[f] = send[k // 2, base : base + ROWS, :] + back * solve_main[f]
            send[k // 2, base : base + ROWS, :] = solve_main[f]
        base = 96 + 8 * (k % 2)
        solve_rest = send[k // 2, base : base + 8, :] + factors_rest[2, k] * solve_rest
        send[k // 2, base : base + 8, :] = solve_rest


def unpack_kernel(received, tracer_out, u_out, v_out):
    lane = lane_ids(ROWS)
    lane8 = lane_ids(8)
    for level in range(2):
        for field, out in enumerate((tracer_out, u_out, v_out)):
            base = (field * 2 + level) * ROWS
            before = None
            for tile in range(LON // LANES):
                source = tile if tile < 8 else tile - 1
                fresh = tile != 8 and tile != 17
                shift = 16 * (source % 8) if fresh else LANES
                value = received[source, base : base + ROWS, :] if fresh else None
                if shift > 0:
                    last = source - 1 if fresh else (7 if tile == 8 else 15)
                    place = shift - 16
                    packed = received[last, 96 + 8 * level : 104 + 8 * level, :]
                    rest = jnp.concatenate(
                        [
                            pltpu.roll(packed, (place - 32 * field - 16 * half) % LANES, 1)
                            for half in range(2)
                        ],
                        axis=0,
                    )
                    old = received[last, base : base + ROWS, :]
                    old = jnp.where(lane >= place, rest, old) if place > 0 else rest
                    value = jnp.where(lane >= shift, value, old) if fresh else old
                out[level, :, tile * LANES : (tile + 1) * LANES] = value


def call(kernel, in_specs, shapes, scratch=(), flops=1000000, nbytes=3000000):
    return pl.pallas_call(
        kernel,
        in_specs=in_specs,
        out_specs=[VM] * len(shapes),
        out_shape=[jax.ShapeDtypeStruct(s, d) for s, d in shapes],
        scratch_shapes=scratch,
        compiler_params=PARAMS,
        cost_estimate=pl.CostEstimate(flops=flops, bytes_accessed=nbytes, transcendentals=0),
    )


def local(tracer, thickness, wind_u, wind_v, offsets, coupling):
    f32, i32 = jnp.float32, jnp.int32
    lat, lev = lax.axis_index("lat"), lax.axis_index("lev")
    lat_count = lax.axis_size("lat")
    slab = (2, ROWS, LON)
    halo = (5, 2, LON)
    winds = (tracer, thickness, wind_u, wind_v)
    to_north, to_south = call(edge_kernel, [VM] * 4, [(halo, f32)] * 2)(*winds)
    up = [(i, i + 1) for i in range(lat_count - 1)]
    south = lax.ppermute(to_north, "lat", up)
    north = lax.ppermute(to_south, "lat", [(b, a) for a, b in up])
    firsts = call(first_kernel, [VM] * 4, [(slab, f32)] * 4)(*winds)
    inside = jnp.stack([lat > 0, lat < lat_count - 1]).astype(f32)
    (send,) = call(
        second_kernel,
        [SM] + [VM] * 10,
        [((DEST, 144, LANES), f32)],
        scratch=[pltpu.VMEM((4,) + slab, f32)],
    )(inside, *winds, *firsts, south, north)
    received = lax.all_to_all(send, "lev", split_axis=0, concat_axis=0, tiled=True)
    shift = (16 * lax.rem(lev, 8)).astype(i32).reshape(1)
    factors = call(
        factor_kernel,
        [SM, VM, VM],
        [
            ((LEVELS, ROWS, LANES), i32),
            ((LEVELS, 8, LANES), i32),
            ((3, LEVELS, ROWS, LANES), f32),
            ((3, LEVELS, 8, LANES), f32),
        ],
    )(shift, offsets, coupling)
    (back,) = call(column_kernel, [VM] * 5, [((DEST, 112, LANES), f32)])(received, *factors)
    returned = lax.all_to_all(back, "lev", split_axis=0, concat_axis=0, tiled=True)
    return tuple(call(unpack_kernel, [VM], [(slab, f32)] * 3)(returned))


def solution(mesh):
    return jax.shard_map(
        local,
        mesh=mesh,
        in_specs=(
            P("lev", "lat", None),
            P("lev", "lat", None),
            P("lev", "lat", None),
            P("lev", "lat", None),
            P(None, "lat", "lev"),
            P(None, "lat", "lev"),
        ),
        out_specs=(P("lev", "lat", None), P("lev", "lat", None), P("lev", "lat", None)),
        check_vma=False,
    )
```

profile of v0, /device:TPU:70, one launch (start us, length us, event | category | flops | bytes accessed | tf_op | source)
XLA Modules:
  0.0 69.0 jit_solution(7552406675286933813)
XLA Ops:
  0.6 0.0 copy-start
  0.6 1.0 %copy-done = f32[2,16,2304]{2,1,0:T(8,128)S(1)} copy-done((f32[2,16,2304]{2,1,0:T(8,128)S(1)}, f32[2,16,2304]{2,1,0:T(8,128)}, u32[]{:S(2)}) %copy-start) | copy-done | bytes 294936
  1.6 1.0 %copy-done.2 = f32[2,16,2304]{2,1,0:T(8,128)S(1)} copy-done((f32[2,16,2304]{2,1,0:T(8,128)S(1)}, f32[2,16,2304]{2,1,0:T(8,128)}, u32[]{:S(2)}) %copy-start.2) | copy-done | bytes 294936
  2.6 1.0 %copy-done.4 = f32[2,16,2304]{2,1,0:T(8,128)S(1)} copy-done((f32[2,16,2304]{2,1,0:T(8,128)S(1)}, f32[2,16,2304]{2,1,0:T(8,128)}, u32[]{:S(2)}) %copy-start.4) | copy-done | bytes 294936
  3.5 1.0 %copy-done.6 = f32[2,16,2304]{2,1,0:T(8,128)S(1)} copy-done((f32[2,16,2304]{2,1,0:T(8,128)S(1)}, f32[2,16,2304]{2,1,0:T(8,128)}, u32[]{:S(2)}) %copy-start.6) | copy-done | bytes 294936
  4.5 0.2 shard_map.86
  4.7 6.4 %collective-permute-start = (f32[5,2,2304]{2,1,0:T(2,128)S(1)}, f32[5,2,2304]{2,1,0:T(2,128)S(1)}, u32[]{:S(2)}, u32[]{:S(2)}) collective-permute-start(f32[5,2,2304]{2,1,0:T(2,128)S(1)} %get-tuple-element.17), channel_id=1, source_target_pairs={{0,16},{16,32},{32,48},{48,64},{64,80},{80,96},{96,112},{112,128},... | collective-permute-start | bytes 276488 | tf_op jit(solution)/shard_map/ppermute | solution.py:282
  11.2 1.9 %collective-permute-start.1 = (f32[5,2,2304]{2,1,0:T(2,128)S(1)}, f32[5,2,2304]{2,1,0:T(2,128)S(1)}, u32[]{:S(2)}, u32[]{:S(2)}) collective-permute-start(f32[5,2,2304]{2,1,0:T(2,128)S(1)} %get-tuple-element.18), channel_id=1, source_target_pairs={{16,0},{32,16},{48,32},{64,48},{80,64},{96,80},{112,96},{128,112},... | collective-permute-start | bytes 276488 | tf_op jit(solution)/shard_map/ppermute | solution.py:283
  13.1 0.8 %shard_map.85 = (f32[2,16,2304]{2,1,0:T(8,128)S(1)}, f32[2,16,2304]{2,1,0:T(8,128)S(1)}, f32[2,16,2304]{2,1,0:T(8,128)S(1)}, f32[2,16,2304]{2,1,0:T(8,128)S(1)}) custom-call(f32[2,16,2304]{2,1,0:T(8,128)S(1)} %copy-done, f32[2,16,2304]{2,1,0:T(8,128)S(1)} %copy-done.2, f32[2,16,2304]{2,1,0:T(8,128)S(1)} %copy-done.4, f32[2,16,2304]{2,1,0:T(8,128)S(1)} %copy-done.6), custom_call_target="tpu_custom_call" | custom-call | flops 1000000 | bytes 3000000 | tf_op jit(solution)/shard_map/pallas_call | solution.py:284
  13.9 0.1 add_convert_fusion.inside
  14.0 0.9 %collective-permute-done.south = f32[5,2,2304]{2,1,0:T(2,128)S(1)} collective-permute-done((f32[5,2,2304]{2,1,0:T(2,128)S(1)}, f32[5,2,2304]{2,1,0:T(2,128)S(1)}, u32[]{:S(2)}, u32[]{:S(2)}) %collective-permute-start) | collective-permute-done | bytes 92192 | tf_op jit(solution)/shard_map/ppermute | solution.py:282
  14.9 8.3 %collective-permute-done.1.north_halo = f32[5,2,2304]{2,1,0:T(2,128)S(1)} collective-permute-done((f32[5,2,2304]{2,1,0:T(2,128)S(1)}, f32[5,2,2304]{2,1,0:T(2,128)S(1)}, u32[]{:S(2)}, u32[]{:S(2)}) %collective-permute-start.1) | collective-permute-done | bytes 92192 | tf_op jit(solution)/shard_map/ppermute | solution.py:283
  23.2 0.0 copy-done.1
  23.2 0.0 copy-done.3
  23.2 2.6 %shard_map.87 = f32[16,144,128]{2,1,0:T(8,128)} custom-call(f32[2]{0:T(128)S(1)} %add_convert_fusion.inside, f32[2,16,2304]{2,1,0:T(8,128)S(1)} %copy-done.1, f32[2,16,2304]{2,1,0:T(8,128)S(1)} %copy-done.3, f32[2,16,2304]{2,1,0:T(8,128)S(1)} %copy-done.5, f32[2,16,2304]{2,1,0:T(8,128)S(1)} %copy-done.7, f32[2,16,2304]{2,1,0:T(8,128)S(1)} %get-tuple-element.13.east_in, ...), custom_call_target="tpu_custom_call" | custom-call | flops 1000000 | bytes 3000000 | tf_op jit(solution)/shard_map/pallas_call | solution.py:286
  25.8 4.9 %all-to-all-start = ((f32[16,144,128]{2,1,0:T(8,128)}), f32[16,144,128]{2,1,0:T(8,128)S(1)}, u32[]{:S(2)}, u32[]{:S(2)}) async-start(f32[16,144,128]{2,1,0:T(8,128)} %shard_map.87), calls=%async_computation | async-start | bytes 2359296 | tf_op jit(solution)/shard_map/all_to_all | solution.py:292
  30.8 1.7 %shard_map.88 = (s32[32,16,128]{2,1,0:T(8,128)S(1)}, s32[32,8,128]{2,1,0:T(8,128)S(1)}, f32[3,32,16,128]{3,2,1,0:T(8,128)S(1)}, f32[3,32,8,128]{3,2,1,0:T(8,128)S(1)}) custom-call(s32[1]{0:T(128)} %bitcast.2.shift_ref, s32[32,16,144]{2,1,0:T(8,128)S(1)} %copy-done.8, f32[31,16,144]{2,1,0:T(8,128)S(1)} %copy-done.9), custom_call_target="tpu_custom_call" | custom-call | flops 1000000 | bytes 3000000 | tf_op jit(solution)/shard_map/pallas_call | solution.py:294
  32.5 0.0 copy-start.10
  32.5 0.7 %copy-done.10 = s32[32,16,128]{2,1,0:T(8,128)} copy-done((s32[32,16,128]{2,1,0:T(8,128)}, s32[32,16,128]{2,1,0:T(8,128)S(1)}, u32[]{:S(2)}) %copy-start.10) | copy-done | bytes 262168
  33.2 15.6 %all-to-all-done.received = f32[16,144,128]{2,1,0:T(8,128)S(1)} async-done(((f32[16,144,128]{2,1,0:T(8,128)}), f32[16,144,128]{2,1,0:T(8,128)S(1)}, u32[]{:S(2)}, u32[]{:S(2)}) %all-to-all-start) | async-done | bytes 1179680 | tf_op jit(solution)/shard_map/all_to_all | solution.py:292
  48.8 0.9 %copy-done.11 = s32[32,16,128]{2,1,0:T(8,128)S(1)} copy-done((s32[32,16,128]{2,1,0:T(8,128)S(1)}, s32[32,16,128]{2,1,0:T(8,128)}, u32[]{:S(2)}) %copy-start.11) | copy-done | bytes 262168
  49.7 0.4 shard_map.89
  50.1 17.8 %all_to_all.10.received = f32[16,112,128]{2,1,0:T(8,128)S(1)} all-to-all(f32[16,112,128]{2,1,0:T(8,128)S(1)} %shard_map.89), channel_id=1, replica_groups=mesh['lat'=16,'lev'=16] {'lev'}, dimensions={0} | all-to-all | bytes 1835008 | tf_op jit(solution)/shard_map/all_to_all | solution.py:305
  67.9 1.1 %shard_map.90 = (f32[2,16,2304]{2,1,0:T(8,128)}, f32[2,16,2304]{2,1,0:T(8,128)}, f32[2,16,2304]{2,1,0:T(8,128)}) custom-call(f32[16,112,128]{2,1,0:T(8,128)S(1)} %all_to_all.10.received), custom_call_target="tpu_custom_call" | custom-call | flops 1000000 | bytes 3000000 | tf_op jit(solution)/shard_map/pallas_call | solution.py:306
  (14 shorter events, 0.0 us)
Async XLA Ops:
  0.6 1.0 %copy-start = (f32[2,16,2304]{2,1,0:T(8,128)S(1)}, f32[2,16,2304]{2,1,0:T(8,128)}, u32[]{:S(2)}) copy-start(f32[2,16,2304]{2,1,0:T(8,128)} %tracer.5) | copy-start | bytes 884740
  1.6 1.0 %copy-start.2 = (f32[2,16,2304]{2,1,0:T(8,128)S(1)}, f32[2,16,2304]{2,1,0:T(8,128)}, u32[]{:S(2)}) copy-start(f32[2,16,2304]{2,1,0:T(8,128)} %thickness.5) | copy-start | bytes 884740
  2.6 1.0 %copy-start.4 = (f32[2,16,2304]{2,1,0:T(8,128)S(1)}, f32[2,16,2304]{2,1,0:T(8,128)}, u32[]{:S(2)}) copy-start(f32[2,16,2304]{2,1,0:T(8,128)} %wind_u.5) | copy-start | bytes 884740
  3.5 1.0 %copy-start.6 = (f32[2,16,2304]{2,1,0:T(8,128)S(1)}, f32[2,16,2304]{2,1,0:T(8,128)}, u32[]{:S(2)}) copy-start(f32[2,16,2304]{2,1,0:T(8,128)} %wind_v.5) | copy-start | bytes 884740
  4.5 18.7 %copy-start.1 = (f32[2,16,2304]{2,1,0:T(8,128)S(1)}, f32[2,16,2304]{2,1,0:T(8,128)}, u32[]{:S(2)}) copy-start(f32[2,16,2304]{2,1,0:T(8,128)} %tracer.5) | copy-start | bytes 884740
  4.5 18.7 %copy-start.3 = (f32[2,16,2304]{2,1,0:T(8,128)S(1)}, f32[2,16,2304]{2,1,0:T(8,128)}, u32[]{:S(2)}) copy-start(f32[2,16,2304]{2,1,0:T(8,128)} %thickness.5) | copy-start | bytes 884740
  4.5 18.7 %copy-start.5 = (f32[2,16,2304]{2,1,0:T(8,128)S(1)}, f32[2,16,2304]{2,1,0:T(8,128)}, u32[]{:S(2)}) copy-start(f32[2,16,2304]{2,1,0:T(8,128)} %wind_u.5) | copy-start | bytes 884740
  4.5 18.7 %copy-start.7 = (f32[2,16,2304]{2,1,0:T(8,128)S(1)}, f32[2,16,2304]{2,1,0:T(8,128)}, u32[]{:S(2)}) copy-start(f32[2,16,2304]{2,1,0:T(8,128)} %wind_v.5) | copy-start | bytes 884740
  4.7 10.2 %collective-permute-start = (f32[5,2,2304]{2,1,0:T(2,128)S(1)}, f32[5,2,2304]{2,1,0:T(2,128)S(1)}, u32[]{:S(2)}, u32[]{:S(2)}) collective-permute-start(f32[5,2,2304]{2,1,0:T(2,128)S(1)} %get-tuple-element.17), channel_id=1, source_target_pairs={{0,16},{16,32},{32,48},{48,64},{64,80},{80,96},{96,112},{112,128},... | collective-permute-start | bytes 276488 | tf_op jit(solution)/shard_map/ppermute | solution.py:282
  11.2 12.0 %collective-permute-start.1 = (f32[5,2,2304]{2,1,0:T(2,128)S(1)}, f32[5,2,2304]{2,1,0:T(2,128)S(1)}, u32[]{:S(2)}, u32[]{:S(2)}) collective-permute-start(f32[5,2,2304]{2,1,0:T(2,128)S(1)} %get-tuple-element.18), channel_id=1, source_target_pairs={{16,0},{32,16},{48,32},{64,48},{80,64},{96,80},{112,96},{128,112},... | collective-permute-start | bytes 276488 | tf_op jit(solution)/shard_map/ppermute | solution.py:283
  25.8 4.9 %copy-start.8 = (s32[32,16,144]{2,1,0:T(8,128)S(1)}, s32[32,16,144]{2,1,0:T(8,128)}, u32[]{:S(2)}) copy-start(s32[32,16,144]{2,1,0:T(8,128)} %offsets.1) | copy-start | bytes 884740
  25.8 4.9 %copy-start.9 = (f32[31,16,144]{2,1,0:T(8,128)S(1)}, f32[31,16,144]{2,1,0:T(8,128)}, u32[]{:S(2)}) copy-start(f32[31,16,144]{2,1,0:T(8,128)} %coupling.1) | copy-start | bytes 857092
  25.8 23.0 %all-to-all-start = ((f32[16,144,128]{2,1,0:T(8,128)}), f32[16,144,128]{2,1,0:T(8,128)S(1)}, u32[]{:S(2)}, u32[]{:S(2)}) async-start(f32[16,144,128]{2,1,0:T(8,128)} %shard_map.87), calls=%async_computation | async-start | bytes 2359296 | tf_op jit(solution)/shard_map/all_to_all | solution.py:292
  32.5 0.7 %copy-start.10 = (s32[32,16,128]{2,1,0:T(8,128)}, s32[32,16,128]{2,1,0:T(8,128)S(1)}, u32[]{:S(2)}) copy-start(s32[32,16,128]{2,1,0:T(8,128)S(1)} %get-tuple-element.19.choose_main) | copy-start | bytes 786436
  48.8 1.0 %copy-start.11 = (s32[32,16,128]{2,1,0:T(8,128)S(1)}, s32[32,16,128]{2,1,0:T(8,128)}, u32[]{:S(2)}) copy-start(s32[32,16,128]{2,1,0:T(8,128)} %copy-done.10) | copy-start | bytes 786436
where the time goes:
time: 69.5 us; the launch traced here: 69 us
  waiting for transfers between devices  24.8 us (36%)
  blocking collectives  17.8 us (26%)
  starting transfers between devices  13.3 us (19%)
  Pallas kernels  6.77 us (10%)
  local copies, waits for them, and re-layouts  5.51 us (8%)
  between operations  0.76 us (1%)
    all_to_all x1, blocking collectives, local(): lax.all_to_all(back, 'lev', split_axis=0, concat_axis=0, tiled=True)  17.8 us
    all_to_all x1, waiting for transfers between devices, local(): lax.all_to_all(send, 'lev', split_axis=0, concat_axis=0, tiled=True)  15.6 us
    ppermute x1, waiting for transfers between devices, local(): north = lax.ppermute(to_south, 'lat', [(b, a) for a, b in up])  8.29 us
    ppermute x1, starting transfers between devices, local(): south = lax.ppermute(to_north, 'lat', up)  6.44 us
    unnamed x24, local copies, waits for them, and re-layouts  5.51 us
    all_to_all x1, starting transfers between devices, local(): lax.all_to_all(send, 'lev', split_axis=0, concat_axis=0, tiled=True)  4.9 us
    pallas_call x1, Pallas kernels, local(): call(second_kernel, [SM] + [VM] * 10, [((DEST, 144, LANES), f32)], scratc...  2.59 us
    ppermute x1, starting transfers between devices, local(): north = lax.ppermute(to_south, 'lat', [(b, a) for a, b in up])  1.92 us
  transfers between devices with their start and end apart: 3, of which 3 were waited for; matrix products, arithmetic and copies ran while one was open for 0% of the time, Pallas kernels for 4%

commit v1 on v0

v1 whole, which is shorter than its diff:
```python
import jax
import jax.numpy as jnp
from jax import lax
from jax.experimental import pallas as pl
from jax.experimental.pallas import tpu as pltpu
from jax.sharding import PartitionSpec as P

courant_max = 0.24
LEVELS = 32
LON = 2304
ROWS = 16
DEST = 16
COLS = 144
LANES = 128
VM = pl.BlockSpec(memory_space=pltpu.VMEM)
ANY = pl.BlockSpec(memory_space=pl.ANY)
HB = pl.BlockSpec(memory_space=pltpu.HBM)
PARAMS = pltpu.CompilerParams(vmem_limit_bytes=24 * 1024 * 1024)


def lane_ids(rows):
    return lax.broadcasted_iota(jnp.int32, (rows, LANES), 1)


def row_ids(rows):
    return lax.broadcasted_iota(jnp.int32, (rows, LON), 0)


def courant(pair_sum):
    return courant_max * jnp.tanh(0.5 * pair_sum)


def upwind(flow, before, after):
    return jnp.maximum(flow, 0.0) * before + jnp.minimum(flow, 0.0) * after


def east_roll(x):
    return pltpu.roll(x, 1, 1)


def west_roll(x):
    return pltpu.roll(x, LON - 1, 1)


def zonal(east, mass):
    flux = upwind(east, east_roll(mass), mass)
    return flux - west_roll(flux)


def edge_kernel(tracer, thickness, wind_u, wind_v, to_first, to_second, kept, fetched, sems):
    copies = []
    for slot, ref in enumerate((tracer, thickness, wind_u, wind_v)):
        for level in range(2):
            for end in range(2):
                copies.append(
                    pltpu.make_async_copy(
                        ref.at[level, pl.ds(14 * end, 2), :],
                        fetched.at[slot, pl.ds(4 * level + 2 * end, 2), :],
                        sems.at[4 * slot + 2 * level + end],
                    )
                )
    for copy in copies:
        copy.start()
    for copy in copies:
        copy.wait()
    layer, u, v = fetched[1], fetched[2], fetched[3]
    mass = fetched[0] * layer
    east = courant(east_roll(u) + u)
    north = courant(v + pltpu.roll(v, 7, 0))
    odd = lax.rem(row_ids(8), 2) == 1
    upper = lax.rem(row_ids(8), 4) >= 2
    inner = jnp.where(odd, pltpu.roll(north, 1, 0), north)

    def partial(m):
        flux = upwind(north, m, pltpu.roll(m, 7, 0))
        return m + zonal(east, m) + jnp.where(odd, pltpu.roll(flux, 1, 0), -flux)

    values = (v, layer, mass, partial(layer), partial(mass))
    odd_lat = lax.rem(lax.axis_index("lat"), 2) == 1
    north_first = jnp.broadcast_to(odd_lat, (1, LON))
    for slot, value in enumerate(values):
        for level in range(2):
            south = value[4 * level : 4 * level + 1]
            north_row = value[4 * level + 3 : 4 * level + 4]
            to_first[slot, level : level + 1, :] = jnp.where(north_first, north_row, south)
            to_second[slot, level : level + 1, :] = jnp.where(north_first, south, north_row)
        kept[slot] = value
    kept[5] = east
    kept[6] = jnp.where(upper, jnp.minimum(inner, 0.0), -jnp.maximum(inner, 0.0))
    kept[7] = u


def first_kernel(tracer, thickness, wind_u, wind_v, send, edges, held, packed_all, sems):
    row = row_ids(ROWS)
    for level in range(2):
        u, v, layer = wind_u[level], wind_v[level], thickness[level]
        mass = tracer[level] * layer
        east = courant(east_roll(u) + u)
        north = jnp.where(row == 0, 0.0, courant(pltpu.roll(v, 1, 0) + v))
        done = []
        for m in (layer, mass):
            for substep in range(2):
                flux = upwind(north, pltpu.roll(m, 1, 0), m)
                above = jnp.where(row == ROWS - 1, 0.0, pltpu.roll(flux, ROWS - 1, 0))
                m = m + zonal(east, m) + flux - above
            done.append(m)
        layer, mass = done
        for slot, m in enumerate(done):
            edges[slot, 4 * level : 4 * level + 2, :] = m[0:2]
            edges[slot, 4 * level + 2 : 4 * level + 4, :] = m[14:16]
        held[0, level] = mass
        held[1, level] = layer * u
        held[2, level] = layer * v
        held[3, level] = layer
    lane = lane_ids(ROWS)
    lane8 = lane_ids(8)
    copies = []
    for dest in range(DEST):
        tile = dest + dest // 8
        shift = 16 * (dest % 8)
        low = slice(tile * LANES, (tile + 1) * LANES)
        high = slice((tile + 1) * LANES, (tile + 2) * LANES)
        for level in range(2):
            packed = None
            for field in range(4):
                here = held[field, level, :, low]
                after = held[field, level, :, high]
                block = here if shift == 0 else jnp.where(lane >= shift, here, after)
                start = (field * 2 + level) * ROWS
                packed_all[dest, start : start + ROWS, :] = block
                for half in range(2):
                    part = after[8 * half : 8 * half + 8]
                    part = pltpu.roll(part, 2, 0) if half else part
                    place = 32 * field + 16 * half
                    part = pltpu.roll(part, (place - shift) % LANES, 1)
                    packed = part if packed is None else jnp.where(lane8 >= place, part, packed)
            packed_all[dest, 128 + 8 * level : 136 + 8 * level, :] = packed
        copy = pltpu.make_async_copy(packed_all.at[dest], send.at[dest], sems.at[dest])
        copy.start()
        copies.append(copy)
    for copy in copies:
        copy.wait()


def second_kernel(first_halo, second_halo, kept, edges, sent, send, held, patch, sems):
    lat = lax.axis_index("lat")
    row = lax.rem(row_ids(8), 4)
    upper = row >= 2
    outer = (row == 0) | (row == 3)
    even = jnp.broadcast_to(lax.rem(lat, 2) == 0, (1, LON))
    south_open = jnp.where(lat > 0, 1.0, 0.0)
    north_open = jnp.where(lat < lax.axis_size("lat") - 1, 1.0, 0.0)
    open_face = jnp.where(upper, north_open, south_open)

    def halo(slot):
        rows = []
        for level in range(2):
            one = first_halo[slot, level : level + 1, :]
            two = second_halo[slot, level : level + 1, :]
            south = jnp.where(even, one, two)
            north = jnp.where(even, two, one)
            rows.append(jnp.where(upper[0:4], north, south))
        return jnp.concatenate(rows, axis=0)

    v, east, inner = kept[0], kept[5], kept[6]
    flow = open_face * courant(v + halo(0))
    sign = jnp.where(upper, -1.0, 1.0)
    done = []
    for slot in range(2):
        m, m_beyond = kept[1 + slot], halo(1 + slot)
        partial, beyond = kept[3 + slot], halo(3 + slot)
        flux = upwind(flow, jnp.where(upper, m, m_beyond), jnp.where(upper, m_beyond, m))
        change = jnp.where(outer, sign * flux, 0.0)
        partial = partial + change
        beyond = beyond - change
        flux = upwind(flow, jnp.where(upper, partial, beyond), jnp.where(upper, beyond, partial))
        carried = inner * change
        gain = change + zonal(east, change) + carried + sign * flux
        passed = jnp.where(row == 1, pltpu.roll(carried, 1, 0), pltpu.roll(carried, 7, 0))
        done.append(edges[slot] + jnp.where(outer, gain, -passed))
    layer, mass = done
    held[0] = mass
    held[1] = layer * kept[7]
    held[2] = layer * v
    held[3] = layer
    lane = lane_ids(8)
    group = lax.rem(lane, 32) < 16
    for dest in range(DEST):
        tile = dest + dest // 8
        shift = 16 * (dest % 8)
        low = slice(tile * LANES, (tile + 1) * LANES)
        high = slice((tile + 1) * LANES, (tile + 2) * LANES)
        packed = None
        for field in range(4):
            here, after = held[field, :, low], held[field, :, high]
            block = here if shift == 0 else jnp.where(lane >= shift, here, after)
            for level in range(2):
                start = (field * 2 + level) * ROWS
                patch[dest, start : start + 2, :] = block[4 * level : 4 * level + 2]
                patch[dest, start + 14 : start + 16, :] = block[4 * level + 2 : 4 * level + 4]
            place = 32 * field
            both = jnp.where(
                group,
                pltpu.roll(after, (place - shift) % LANES, 1),
                pltpu.roll(pltpu.roll(after, 6, 0), (place + 16 - shift) % LANES, 1),
            )
            packed = both if field == 0 else jnp.where(lane >= place, both, packed)
        for level in range(2):
            start = 128 + 8 * level
            patch[dest, start : start + 2, :] = packed[4 * level : 4 * level + 2]
    spots = [16 * i + end for i in range(8) for end in (0, 14)] + [128, 136]
    copies = [
        pltpu.make_async_copy(
            patch.at[:, pl.ds(spot, 2), :], send.at[:, pl.ds(spot, 2), :], sems.at[i]
        )
        for i, spot in enumerate(spots)
    ]
    for copy in copies:
        copy.start()
    for copy in copies:
        copy.wait()


def factor_kernel(offsets, coupling, factors_main, factors_rest):
    shift = 16 * lax.rem(lax.axis_index("lev"), 8)
    half = lax.rem(lane_ids(8), 32) >= 16

    def main(ref, k):
        return pltpu.roll(ref[k, :, 0:LANES], shift, 1)

    def rest(ref, k):
        part = ref[k, :, LANES:COLS]
        both = jnp.concatenate([part[0:8], part[8:16]], axis=1)
        all_fields = jnp.concatenate([both, both, both, both], axis=1)
        return jnp.where(half, pltpu.roll(all_fields, 2, 0), all_fields)

    for load, factors, shape in (
        (main, factors_main, (ROWS, LANES)),
        (rest, factors_rest, (8, LANES)),
    ):
        low = jnp.zeros(shape, jnp.float32)
        back = jnp.zeros(shape, jnp.float32)
        for k in range(LEVELS):
            choose = load(offsets, k)
            high = load(coupling, k) if k < LEVELS - 1 else jnp.zeros(shape, jnp.float32)
            scale = 1.0 / (1.0 + low + high - low * back)
            back = high * scale
            factors[0, k] = jnp.where(choose == 0, -scale, scale)
            factors[1, k] = low * scale
            factors[2, k] = jnp.where(choose == 2, -back, back)
            low = high


def column_kernel(received, factors_main, factors_rest, send):
    lane = lane_ids(8)

    def main(k):
        base = (k % 2) * ROWS
        return [received[k // 2, base + 32 * f : base + 32 * f + ROWS, :] for f in range(4)]

    def rest(k):
        base = 128 + 8 * (k % 2)
        return received[k // 2, base : base + 8, :]

    def picked(below, above, sums):
        return jnp.where(below, sums[0], jnp.where(above, sums[2], sums[1]))

    solve_main = [jnp.zeros((ROWS, LANES), jnp.float32)] * 3
    solve_rest = jnp.zeros((8, LANES), jnp.float32)
    main_here, rest_here = main(0), rest(0)
    main_sums, rest_sums = [], []

    def push(k):
        nonlocal main_here, rest_here
        main_next, rest_next = main(k + 1), rest(k + 1)
        main_sums.append([a + b for a, b in zip(main_here, main_next)])
        rest_sums.append(rest_here + rest_next)
        main_here, rest_here = main_next, rest_next

    push(0)
    for k in range(LEVELS):
        if k + 1 < LEVELS - 1:
            push(k + 1)
        three = [max(k - 1, 0), min(k, LEVELS - 2), min(k + 1, LEVELS - 2)]
        scale = factors_main[0, k]
        below, above = scale < 0.0, factors_main[2, k] < 0.0
        values = [picked(below, above, [main_sums[i][f] for i in three]) for f in range(4)]
        weight = jnp.abs(scale) / values[3]
        low = factors_main[1, k]
        solve_main = [values[f] * weight + low * solve_main[f] for f in range(3)]
        for f in range(3):
            base = (f * 2 + k % 2) * ROWS
            send[k // 2, base : base + ROWS, :] = solve_main[f]
        scale = factors_rest[0, k]
        below, above = scale < 0.0, factors_rest[2, k] < 0.0
        value = picked(below, above, [rest_sums[i] for i in three])
        total = jnp.where(lane >= 64, pltpu.roll(value, 96, 1), pltpu.roll(value, 32, 1))
        total = jnp.where(lane >= 32, jnp.where(lane >= 64, total, pltpu.roll(value, 64, 1)), total)
        solve_rest = value * (jnp.abs(scale) / total) + factors_rest[1, k] * solve_rest
        base = 96 + 8 * (k % 2)
        send[k // 2, base : base + 8, :] = solve_rest
    for k in range(LEVELS - 2, -1, -1):
        back = jnp.abs(factors_main[2, k])
        for f in range(3):
            base = (f * 2 + k % 2) * ROWS
            solve_main[f] = send[k // 2, base : base + ROWS, :] + back * solve_main[f]
            send[k // 2, base : base + ROWS, :] = solve_main[f]
        base = 96 + 8 * (k % 2)
        solve_rest = send[k // 2, base : base + 8, :] + jnp.abs(factors_rest[2, k]) * solve_rest
        send[k // 2, base : base + 8, :] = solve_rest


def unpack_kernel(received, tracer_out, u_out, v_out, whole, sems):
    lane = lane_ids(ROWS)
    copies = []
    for field, out in enumerate((tracer_out, u_out, v_out)):
        for level in range(2):
            base = (field * 2 + level) * ROWS
            for tile in range(LON // LANES):
                source = tile if tile < 8 else tile - 1
                fresh = tile != 8 and tile != 17
                shift = 16 * (source % 8) if fresh else LANES
                value = received[source, base : base + ROWS, :] if fresh else None
                if shift > 0:
                    last = source - 1 if fresh else (7 if tile == 8 else 15)
                    place = shift - 16
                    packed = received[last, 96 + 8 * level : 104 + 8 * level, :]
                    start = place - 32 * field
                    rest = jnp.concatenate(
                        [
                            pltpu.roll(packed, start % LANES, 1),
                            pltpu.roll(pltpu.roll(packed, 6, 0), (start - 16) % LANES, 1),
                        ],
                        axis=0,
                    )
                    old = received[last, base : base + ROWS, :]
                    old = jnp.where(lane >= place, rest, old) if place > 0 else rest
                    value = jnp.where(lane >= shift, value, old) if fresh else old
                whole[field, level, :, tile * LANES : (tile + 1) * LANES] = value
            copy = pltpu.make_async_copy(
                whole.at[field, level], out.at[level], sems.at[2 * field + level]
            )
            copy.start()
            copies.append(copy)
    for copy in copies:
        copy.wait()


def call(kernel, in_specs, outs, scratch=(), aliases=None, flops=1000000, nbytes=3000000):
    return pl.pallas_call(
        kernel,
        in_specs=in_specs,
        out_specs=[spec for spec, _ in outs],
        out_shape=[jax.ShapeDtypeStruct(shape, jnp.float32) for _, shape in outs],
        scratch_shapes=scratch,
        input_output_aliases=aliases or {},
        compiler_params=PARAMS,
        cost_estimate=pl.CostEstimate(flops=flops, bytes_accessed=nbytes, transcendentals=0),
    )


def local(tracer, thickness, wind_u, wind_v, offsets, coupling):
    f32 = jnp.float32
    lat_count = lax.axis_size("lat")
    slab = (2, ROWS, LON)
    halo = (5, 2, LON)
    chunks = (DEST, 144, LANES)
    winds = (tracer, thickness, wind_u, wind_v)
    to_first, to_second, kept = call(
        edge_kernel,
        [HB] * 4,
        [(VM, halo), (VM, halo), (VM, (8, 8, LON))],
        scratch=[pltpu.VMEM((4, 8, LON), f32), pltpu.SemaphoreType.DMA((16,))],
    )(*[pltpu.with_memory_space_constraint(x, pltpu.HBM) for x in winds])
    pairs = [[(i, i + 1) for i in range(start, lat_count - 1, 2)] for start in (1, 0)]
    first_halo, second_halo = [
        lax.ppermute(rows, "lat", [p for a, b in pair for p in ((a, b), (b, a))])
        for rows, pair in zip((to_first, to_second), pairs)
    ]
    send, edges = call(
        first_kernel,
        [VM] * 4,
        [(ANY, chunks), (VM, (2, 8, LON))],
        scratch=[
            pltpu.VMEM((4,) + slab, f32),
            pltpu.VMEM(chunks, f32),
            pltpu.SemaphoreType.DMA((DEST,)),
        ],
    )(*winds)
    (send,) = call(
        second_kernel,
        [VM] * 4 + [ANY],
        [(ANY, chunks)],
        scratch=[
            pltpu.VMEM((4, 8, LON), f32),
            pltpu.VMEM(chunks, f32),
            pltpu.SemaphoreType.DMA((18,)),
        ],
        aliases={4: 0},
    )(first_halo, second_halo, kept, edges, send)
    received = lax.all_to_all(send, "lev", split_axis=0, concat_axis=0, tiled=True)
    factors = call(
        factor_kernel,
        [VM, VM],
        [(VM, (3, LEVELS, ROWS, LANES)), (VM, (3, LEVELS, 8, LANES))],
    )(offsets, coupling)
    (back,) = call(column_kernel, [VM] * 3, [(VM, (DEST, 112, LANES))])(received, *factors)
    returned = lax.all_to_all(back, "lev", split_axis=0, concat_axis=0, tiled=True)
    return tuple(
        call(
            unpack_kernel,
            [VM],
            [(ANY, slab)] * 3,
            scratch=[pltpu.VMEM((3,) + slab, f32), pltpu.SemaphoreType.DMA((6,))],
        )(returned)
    )


def solution(mesh):
    return jax.shard_map(
        local,
        mesh=mesh,
        in_specs=(
            P("lev", "lat", None),
            P("lev", "lat", None),
            P("lev", "lat", None),
            P("lev", "lat", None),
            P(None, "lat", "lev"),
            P(None, "lat", "lev"),
        ),
        out_specs=(P("lev", "lat", None), P("lev", "lat", None), P("lev", "lat", None)),
        check_vma=False,
    )
```

time: 69.5 us -> 58.4 us (0.84)
  local copies, waits for them, and re-layouts: 5.51 us -> 0.03 us
  waiting for transfers between devices: 24.8 us -> 19.8 us
  starting transfers between devices: 13.3 us -> 11.1 us
  Pallas kernels: 6.77 us -> 8.67 us
    ppermute x2, waiting for transfers between devices: 9.19 us -> 3.48 us  [local(): lax.ppermute(rows, 'lat', [p for a, b in pair for p in ((a, b), (b, a))])]
    unnamed x24 -> x12, local copies, waits for them, and re-layouts: 5.51 us -> 0.03 us
    ppermute x2, starting transfers between devices: 8.36 us -> 6.4 us  [local(): lax.ppermute(rows, 'lat', [p for a, b in pair for p in ((a, b), (b, a))])]
    pallas_call x6, Pallas kernels: 6.77 us -> 8.67 us  [the longest x1 2.7 us: local(): call(first_kernel, [VM] * 4, [(ANY, chunks), (VM, (2, 8, LON))], scratch=...]
  transfers between devices with their start and end apart: 3 -> 3, of which waited for: 3 -> 2; matrix products, arithmetic and copies ran while one was open for 0% -> 0% of each run, Pallas kernels for 4% -> 8%
where the time goes in v1:
time: 58.4 us; the launch traced here: 58.2 us
  waiting for transfers between devices  19.8 us (34%)
  blocking collectives  17.8 us (30%)
  starting transfers between devices  11.1 us (19%)
  Pallas kernels  8.67 us (15%)
  between operations  0.79 us (1%)
    all_to_all x1, blocking collectives, local(): lax.all_to_all(back, 'lev', split_axis=0, concat_axis=0, tiled=True)  17.8 us
    all_to_all x1, waiting for transfers between devices, local(): lax.all_to_all(send, 'lev', split_axis=0, concat_axis=0, tiled=True)  16.3 us
    ppermute x2, starting transfers between devices, local(): lax.ppermute(rows, 'lat', [p for a, b in pair for p in ((a, b), (b, a))])  6.4 us
    all_to_all x1, starting transfers between devices, local(): lax.all_to_all(send, 'lev', split_axis=0, concat_axis=0, tiled=True)  4.72 us
    ppermute x2, waiting for transfers between devices, local(): lax.ppermute(rows, 'lat', [p for a, b in pair for p in ((a, b), (b, a))])  3.48 us
    pallas_call x1, Pallas kernels, local(): call(first_kernel, [VM] * 4, [(ANY, chunks), (VM, (2, 8, LON))], scratch=...  2.7 us
    pallas_call x1, Pallas kernels, local(): call(factor_kernel, [VM, VM], [(VM, (3, LEVELS, ROWS, LANES)), (VM, (3, L...  1.75 us
    pallas_call x1, Pallas kernels, local(): call(second_kernel, [VM] * 4 + [ANY], [(ANY, chunks)], scratch=[pltpu.VME...  1.42 us
  transfers between devices with their start and end apart: 3, of which 2 were waited for; matrix products, arithmetic and copies ran while one was open for 0% of the time, Pallas kernels for 8%

profile of v1, /device:TPU:70, one launch (start us, length us, event | category | flops | bytes accessed | tf_op | source)
XLA Modules:
  0.0 58.2 jit_solution(6658284978415223204)
XLA Ops:
  0.6 0.0 copy-start
  0.6 0.0 copy-start.1
  0.7 0.0 copy-start.2
  0.7 0.0 copy-start.3
  0.7 1.4 %shard_map.85 = (f32[5,2,2304]{2,1,0:T(2,128)S(1)}, f32[5,2,2304]{2,1,0:T(2,128)S(1)}, f32[8,8,2304]{2,1,0:T(8,128)S(1)}) custom-call(f32[2,16,2304]{2,1,0:T(8,128)} %tracer.3, f32[2,16,2304]{2,1,0:T(8,128)} %thickness.3, f32[2,16,2304]{2,1,0:T(8,128)} %wind_u.3, f32[2,16,2304]{2,1,0:T(8,128)} %wind_v.3), custom_call_target="tpu_custom_call" | custom-call | flops 1000000 | bytes 3000000 | tf_op jit(solution)/shard_map/pallas_call | solution.py:369
  2.0 6.3 %collective-permute-start = (f32[5,2,2304]{2,1,0:T(2,128)S(1)}, f32[5,2,2304]{2,1,0:T(2,128)S(1)}, u32[]{:S(2)}, u32[]{:S(2)}) collective-permute-start(f32[5,2,2304]{2,1,0:T(2,128)S(1)} %get-tuple-element.10), channel_id=1, source_target_pairs={{16,32},{32,16},{48,64},{64,48},{80,96},{96,80},{112,128},{128,112... | collective-permute-start | bytes 276488 | tf_op jit(solution)/shard_map/ppermute | solution.py:377
  8.4 0.1 collective-permute-start.1
  8.5 0.0 copy-done
  8.5 0.0 copy-done.1
  8.5 0.0 copy-done.2
  8.5 0.0 copy-done.3
  8.5 2.7 %shard_map.86 = (f32[16,144,128]{2,1,0:T(8,128)}, f32[2,8,2304]{2,1,0:T(8,128)S(1)}) custom-call(f32[2,16,2304]{2,1,0:T(8,128)S(1)} %copy-done, f32[2,16,2304]{2,1,0:T(8,128)S(1)} %copy-done.1, f32[2,16,2304]{2,1,0:T(8,128)S(1)} %copy-done.2, f32[2,16,2304]{2,1,0:T(8,128)S(1)} %copy-done.3), custom_call_target="tpu_custom_call" | custom-call | flops 1000000 | bytes 3000000 | tf_op jit(solution)/shard_map/pallas_call | solution.py:380
  11.2 3.5 %collective-permute-done.first_halo = f32[5,2,2304]{2,1,0:T(2,128)S(1)} collective-permute-done((f32[5,2,2304]{2,1,0:T(2,128)S(1)}, f32[5,2,2304]{2,1,0:T(2,128)S(1)}, u32[]{:S(2)}, u32[]{:S(2)}) %collective-permute-start) | collective-permute-done | bytes 92192 | tf_op jit(solution)/shard_map/ppermute | solution.py:377
  14.7 0.0 collective-permute-done.1.second_halo
  14.7 1.4 %shard_map.87 = f32[16,144,128]{2,1,0:T(8,128)} custom-call(f32[5,2,2304]{2,1,0:T(2,128)S(1)} %collective-permute-done.first_halo, f32[5,2,2304]{2,1,0:T(2,128)S(1)} %collective-permute-done.1.second_halo, f32[8,8,2304]{2,1,0:T(8,128)S(1)} %get-tuple-element.12.kept, f32[2,8,2304]{2,1,0:T(8,128)S(1)} %get-tuple-element.13.edges, ...), custom_call_target="tpu_custom_call", output_to_operand_aliasing={{}: (4, {})} | custom-call | flops 1000000 | bytes 3000000 | tf_op jit(solution)/shard_map/pallas_call | solution.py:390
  16.1 0.0 copy-start.4
  16.1 0.0 copy-start.5
  16.1 4.7 %all-to-all-start = ((f32[16,144,128]{2,1,0:T(8,128)}), f32[16,144,128]{2,1,0:T(8,128)S(1)}, u32[]{:S(2)}, u32[]{:S(2)}) async-start(f32[16,144,128]{2,1,0:T(8,128)} %shard_map.87), calls=%async_computation | async-start | bytes 2359296 | tf_op jit(solution)/shard_map/all_to_all | solution.py:401
  20.9 0.0 copy-done.4
  20.9 1.8 %shard_map.88 = (f32[3,32,16,128]{3,2,1,0:T(8,128)S(1)}, f32[3,32,8,128]{3,2,1,0:T(8,128)S(1)}) custom-call(s32[32,16,144]{2,1,0:T(8,128)S(1)} %copy-done.4, f32[31,16,144]{2,1,0:T(8,128)S(1)} %copy-done.5), custom_call_target="tpu_custom_call" | custom-call | flops 1000000 | bytes 3000000 | tf_op jit(solution)/shard_map/pallas_call | solution.py:402
  22.6 16.3 %all-to-all-done.received = f32[16,144,128]{2,1,0:T(8,128)S(1)} async-done(((f32[16,144,128]{2,1,0:T(8,128)}), f32[16,144,128]{2,1,0:T(8,128)S(1)}, u32[]{:S(2)}, u32[]{:S(2)}) %all-to-all-start) | async-done | bytes 1179680 | tf_op jit(solution)/shard_map/all_to_all | solution.py:401
  38.9 0.4 shard_map.89
  39.3 17.8 %all_to_all.10.received = f32[16,112,128]{2,1,0:T(8,128)S(1)} all-to-all(f32[16,112,128]{2,1,0:T(8,128)S(1)} %shard_map.89), channel_id=1, replica_groups=mesh['lat'=16,'lev'=16] {'lev'}, dimensions={0} | all-to-all | bytes 1835008 | tf_op jit(solution)/shard_map/all_to_all | solution.py:408
  57.1 1.1 %shard_map.90 = (f32[2,16,2304]{2,1,0:T(8,128)}, f32[2,16,2304]{2,1,0:T(8,128)}, f32[2,16,2304]{2,1,0:T(8,128)}) custom-call(f32[16,112,128]{2,1,0:T(8,128)S(1)} %all_to_all.10.received), custom_call_target="tpu_custom_call" | custom-call | flops 1000000 | bytes 3000000 | tf_op jit(solution)/shard_map/pallas_call | solution.py:410
  (1 shorter events, 0.0 us)
Async XLA Ops:
  0.6 7.8 %copy-start = (f32[2,16,2304]{2,1,0:T(8,128)S(1)}, f32[2,16,2304]{2,1,0:T(8,128)}, u32[]{:S(2)}) copy-start(f32[2,16,2304]{2,1,0:T(8,128)} %tracer.3) | copy-start | bytes 884740
  0.6 7.8 %copy-start.1 = (f32[2,16,2304]{2,1,0:T(8,128)S(1)}, f32[2,16,2304]{2,1,0:T(8,128)}, u32[]{:S(2)}) copy-start(f32[2,16,2304]{2,1,0:T(8,128)} %thickness.3) | copy-start | bytes 884740
  0.7 7.8 %copy-start.2 = (f32[2,16,2304]{2,1,0:T(8,128)S(1)}, f32[2,16,2304]{2,1,0:T(8,128)}, u32[]{:S(2)}) copy-start(f32[2,16,2304]{2,1,0:T(8,128)} %wind_u.3) | copy-start | bytes 884740
  0.7 7.8 %copy-start.3 = (f32[2,16,2304]{2,1,0:T(8,128)S(1)}, f32[2,16,2304]{2,1,0:T(8,128)}, u32[]{:S(2)}) copy-start(f32[2,16,2304]{2,1,0:T(8,128)} %wind_v.3) | copy-start | bytes 884740
  2.0 12.6 %collective-permute-start = (f32[5,2,2304]{2,1,0:T(2,128)S(1)}, f32[5,2,2304]{2,1,0:T(2,128)S(1)}, u32[]{:S(2)}, u32[]{:S(2)}) collective-permute-start(f32[5,2,2304]{2,1,0:T(2,128)S(1)} %get-tuple-element.10), channel_id=1, source_target_pairs={{16,32},{32,16},{48,64},{64,48},{80,96},{96,80},{112,128},{128,112... | collective-permute-start | bytes 276488 | tf_op jit(solution)/shard_map/ppermute | solution.py:377
  8.4 6.3 %collective-permute-start.1 = (f32[5,2,2304]{2,1,0:T(2,128)S(1)}, f32[5,2,2304]{2,1,0:T(2,128)S(1)}, u32[]{:S(2)}, u32[]{:S(2)}) collective-permute-start(f32[5,2,2304]{2,1,0:T(2,128)S(1)} %get-tuple-element.11), channel_id=1, source_target_pairs={{0,16},{16,0},{32,48},{48,32},{64,80},{80,64},{96,112},{112,96},{1... | collective-permute-start | bytes 276488 | tf_op jit(solution)/shard_map/ppermute | solution.py:377
  16.1 4.8 %copy-start.4 = (s32[32,16,144]{2,1,0:T(8,128)S(1)}, s32[32,16,144]{2,1,0:T(8,128)}, u32[]{:S(2)}) copy-start(s32[32,16,144]{2,1,0:T(8,128)} %offsets.1) | copy-start | bytes 884740
  16.1 4.8 %copy-start.5 = (f32[31,16,144]{2,1,0:T(8,128)S(1)}, f32[31,16,144]{2,1,0:T(8,128)}, u32[]{:S(2)}) copy-start(f32[31,16,144]{2,1,0:T(8,128)} %coupling.1) | copy-start | bytes 857092
  16.1 22.8 %all-to-all-start = ((f32[16,144,128]{2,1,0:T(8,128)}), f32[16,144,128]{2,1,0:T(8,128)S(1)}, u32[]{:S(2)}, u32[]{:S(2)}) async-start(f32[16,144,128]{2,1,0:T(8,128)} %shard_map.87), calls=%async_computation | async-start | bytes 2359296 | tf_op jit(solution)/shard_map/all_to_all | solution.py:401

commit v2 on v1

--- a/solution.py
+++ b/solution.py
@@ -48,23 +48,23 @@
 
 
 def edge_kernel(tracer, thickness, wind_u, wind_v, to_first, to_second, kept, fetched, sems):
-    copies = []
-    for slot, ref in enumerate((tracer, thickness, wind_u, wind_v)):
-        for level in range(2):
-            for end in range(2):
-                copies.append(
-                    pltpu.make_async_copy(
-                        ref.at[level, pl.ds(14 * end, 2), :],
-                        fetched.at[slot, pl.ds(4 * level + 2 * end, 2), :],
-                        sems.at[4 * slot + 2 * level + end],
-                    )
-                )
+    copies = [
+        pltpu.make_async_copy(
+            ref.at[:, pl.ds(14 * end, 2), :],
+            fetched.at[slot, :, pl.ds(2 * end, 2), :],
+            sems.at[2 * slot + end],
+        )
+        for slot, ref in enumerate((tracer, thickness, wind_u, wind_v))
+        for end in range(2)
+    ]
     for copy in copies:
         copy.start()
     for copy in copies:
         copy.wait()
-    layer, u, v = fetched[1], fetched[2], fetched[3]
-    mass = fetched[0] * layer
+    tracer, layer, u, v = [
+        jnp.concatenate([fetched[slot, 0], fetched[slot, 1]], axis=0) for slot in range(4)
+    ]
+    mass = tracer * layer
     east = courant(east_roll(u) + u)
     north = courant(v + pltpu.roll(v, 7, 0))
     odd = lax.rem(row_ids(8), 2) == 1
@@ -75,7 +75,7 @@
         flux = upwind(north, m, pltpu.roll(m, 7, 0))
         return m + zonal(east, m) + jnp.where(odd, pltpu.roll(flux, 1, 0), -flux)
 
-    values = (v, layer, mass, partial(layer), partial(mass))
+    values = (v, mass, layer, partial(mass), partial(layer))
     odd_lat = lax.rem(lax.axis_index("lat"), 2) == 1
     north_first = jnp.broadcast_to(odd_lat, (1, LON))
     for slot, value in enumerate(values):
@@ -87,59 +87,58 @@
         kept[slot] = value
     kept[5] = east
     kept[6] = jnp.where(upper, jnp.minimum(inner, 0.0), -jnp.maximum(inner, 0.0))
-    kept[7] = u
-
-
-def first_kernel(tracer, thickness, wind_u, wind_v, send, edges, held, packed_all, sems):
+
+
+def pack_pair(load, store, places):
+    lane = lane_ids(ROWS)
+    lane8 = lane_ids(8)
+    for dest in range(DEST):
+        tile = dest + dest // 8
+        shift = 16 * (dest % 8)
+        packed = None
+        for place, field, level in places:
+            here, after = load(field, level, tile), load(field, level, tile + 1)
+            block = here if shift == 0 else jnp.where(lane >= shift, here, after)
+            store(dest, (field * 2 + level) * ROWS, block)
+            for half in range(2):
+                part = after[8 * half : 8 * half + 8]
+                part = pltpu.roll(part, 2, 0) if half else part
+                start = place + 16 * half
+                part = pltpu.roll(part, (start - shift) % LANES, 1)
+                packed = part if packed is None else jnp.where(lane8 >= start, part, packed)
+        store(dest, 64, packed)
+
+
+def first_kernel(tracer, thickness, wind_u, wind_v, send, edges, held):
     row = row_ids(ROWS)
     for level in range(2):
         u, v, layer = wind_u[level], wind_v[level], thickness[level]
         mass = tracer[level] * layer
         east = courant(east_roll(u) + u)
         north = jnp.where(row == 0, 0.0, courant(pltpu.roll(v, 1, 0) + v))
-        done = []
-        for m in (layer, mass):
+        for slot, m in enumerate((mass, layer)):
             for substep in range(2):
                 flux = upwind(north, pltpu.roll(m, 1, 0), m)
                 above = jnp.where(row == ROWS - 1, 0.0, pltpu.roll(flux, ROWS - 1, 0))
                 m = m + zonal(east, m) + flux - above
-            done.append(m)
-        layer, mass = done
-        for slot, m in enumerate(done):
             edges[slot, 4 * level : 4 * level + 2, :] = m[0:2]
             edges[slot, 4 * level + 2 : 4 * level + 4, :] = m[14:16]
-        held[0, level] = mass
-        held[1, level] = layer * u
-        held[2, level] = layer * v
-        held[3, level] = layer
-    lane = lane_ids(ROWS)
-    lane8 = lane_ids(8)
-    copies = []
-    for dest in range(DEST):
-        tile = dest + dest // 8
-        shift = 16 * (dest % 8)
-        low = slice(tile * LANES, (tile + 1) * LANES)
-        high = slice((tile + 1) * LANES, (tile + 2) * LANES)
-        for level in range(2):
-            packed = None
-            for field in range(4):
-                here = held[field, level, :, low]
-                after = held[field, level, :, high]
-                block = here if shift == 0 else jnp.where(lane >= shift, here, after)
-                start = (field * 2 + level) * ROWS
-                packed_all[dest, start : start + ROWS, :] = block
-                for half in range(2):
-                    part = after[8 * half : 8 * half + 8]
-                    part = pltpu.roll(part, 2, 0) if half else part
-                    place = 32 * field + 16 * half
-                    part = pltpu.roll(part, (place - shift) % LANES, 1)
-                    packed = part if packed is None else jnp.where(lane8 >= place, part, packed)
-            packed_all[dest, 128 + 8 * level : 136 + 8 * level, :] = packed
-        copy = pltpu.make_async_copy(packed_all.at[dest], send.at[dest], sems.at[dest])
-        copy.start()
-        copies.append(copy)
-    for copy in copies:
-        copy.wait()
+            held[slot, level] = m
+
+    def load(field, level, tile):
+        return held[field, level, :, tile * LANES : (tile + 1) * LANES]
+
+    def load_wind(field, level, tile):
+        return (wind_u, wind_v)[field][level, :, tile * LANES : (tile + 1) * LANES]
+
+    def store(dest, row, value):
+        send[dest, row : row + value.shape[0], :] = value
+
+    def store_wind(dest, row, value):
+        store(dest, 72 + row, value)
+
+    pack_pair(load, store, ((0, 0, 0), (32, 1, 0), (64, 0, 1), (96, 1, 1)))
+    pack_pair(load_wind, store_wind, ((0, 1, 1), (32, 0, 0), (64, 1, 0), (96, 0, 1)))
 
 
 def second_kernel(first_halo, second_halo, kept, edges, sent, send, held, patch, sems):
@@ -165,7 +164,6 @@
     v, east, inner = kept[0], kept[5], kept[6]
     flow = open_face * courant(v + halo(0))
     sign = jnp.where(upper, -1.0, 1.0)
-    done = []
     for slot in range(2):
         m, m_beyond = kept[1 + slot], halo(1 + slot)
         partial, beyond = kept[3 + slot], halo(3 + slot)
@@ -177,38 +175,28 @@
         carried = inner * change
         gain = change + zonal(east, change) + carried + sign * flux
         passed = jnp.where(row == 1, pltpu.roll(carried, 1, 0), pltpu.roll(carried, 7, 0))
-        done.append(edges[slot] + jnp.where(outer, gain, -passed))
-    layer, mass = done
-    held[0] = mass
-    held[1] = layer * kept[7]
-    held[2] = layer * v
-    held[3] = layer
+        held[slot] = edges[slot] + jnp.where(outer, gain, -passed)
     lane = lane_ids(8)
-    group = lax.rem(lane, 32) < 16
     for dest in range(DEST):
         tile = dest + dest // 8
         shift = 16 * (dest % 8)
         low = slice(tile * LANES, (tile + 1) * LANES)
         high = slice((tile + 1) * LANES, (tile + 2) * LANES)
         packed = None
-        for field in range(4):
-            here, after = held[field, :, low], held[field, :, high]
-            block = here if shift == 0 else jnp.where(lane >= shift, here, after)
-            for level in range(2):
+        for level in range(2):
+            for field in range(2):
+                here, after = held[field, :, low], held[field, :, high]
+                block = here if shift == 0 else jnp.where(lane >= shift, here, after)
                 start = (field * 2 + level) * ROWS
                 patch[dest, start : start + 2, :] = block[4 * level : 4 * level + 2]
                 patch[dest, start + 14 : start + 16, :] = block[4 * level + 2 : 4 * level + 4]
-            place = 32 * field
-            both = jnp.where(
-                group,
-                pltpu.roll(after, (place - shift) % LANES, 1),
-                pltpu.roll(pltpu.roll(after, 6, 0), (place + 16 - shift) % LANES, 1),
-            )
-            packed = both if field == 0 else jnp.where(lane >= place, both, packed)
-        for level in range(2):
-            start = 128 + 8 * level
-            patch[dest, start : start + 2, :] = packed[4 * level : 4 * level + 2]
-    spots = [16 * i + end for i in range(8) for end in (0, 14)] + [128, 136]
+                for half in range(2):
+                    start = 64 * level + 32 * field + 16 * half
+                    part = pltpu.roll(after, (8 - 4 * level - 2 * half) % 8, 0)
+                    part = pltpu.roll(part, (start - shift) % LANES, 1)
+                    packed = part if packed is None else jnp.where(lane >= start, part, packed)
+        patch[dest, 64:66, :] = packed[0:2]
+    spots = [16 * i + end for i in range(4) for end in (0, 14)] + [64]
     copies = [
         pltpu.make_async_copy(
             patch.at[:, pl.ds(spot, 2), :], send.at[:, pl.ds(spot, 2), :], sems.at[i]
@@ -252,15 +240,21 @@
 
 
 def column_kernel(received, factors_main, factors_rest, send):
-    lane = lane_ids(8)
+    group = lane_ids(8) // 32
 
     def main(k):
         base = (k % 2) * ROWS
-        return [received[k // 2, base + 32 * f : base + 32 * f + ROWS, :] for f in range(4)]
+        mass, layer = [received[k // 2, base + 32 * f : base + 32 * f + ROWS, :] for f in range(2)]
+        u, v = [received[k // 2, base + 72 + 32 * f : base + 72 + 32 * f + ROWS, :] for f in range(2)]
+        return [mass, layer * u, layer * v, layer]
 
     def rest(k):
-        base = 128 + 8 * (k % 2)
-        return received[k // 2, base : base + 8, :]
+        mass, wind = received[k // 2, 64:72, :], received[k // 2, 136:144, :]
+        if k % 2:
+            mass, wind = pltpu.roll(mass, 64, 1), pltpu.roll(wind, 64, 1)
+        layer = jnp.where(group == 0, pltpu.roll(mass, 96, 1), mass)
+        layer = jnp.where(group >= 2, pltpu.roll(layer, 64, 1), layer)
+        return [jnp.where(group == 0, mass, layer * wind), layer]
 
     def picked(below, above, sums):
         return jnp.where(below, sums[0], jnp.where(above, sums[2], sums[1]))
@@ -274,7 +268,7 @@
         nonlocal main_here, rest_here
         main_next, rest_next = main(k + 1), rest(k + 1)
         main_sums.append([a + b for a, b in zip(main_here, main_next)])
-        rest_sums.append(rest_here + rest_next)
+        rest_sums.append([a + b for a, b in zip(rest_here, rest_next)])
         main_here, rest_here = main_next, rest_next
 
     push(0)
@@ -293,9 +287,7 @@
             send[k // 2, base : base + ROWS, :] = solve_main[f]
         scale = factors_rest[0, k]
         below, above = scale < 0.0, factors_rest[2, k] < 0.0
-        value = picked(below, above, [rest_sums[i] for i in three])
-        total = jnp.where(lane >= 64, pltpu.roll(value, 96, 1), pltpu.roll(value, 32, 1))
-        total = jnp.where(lane >= 32, jnp.where(lane >= 64, total, pltpu.roll(value, 64, 1)), total)
+        value, total = [picked(below, above, [rest_sums[i][f] for i in three]) for f in range(2)]
         solve_rest = value * (jnp.abs(scale) / total) + factors_rest[1, k] * solve_rest
         base = 96 + 8 * (k % 2)
         send[k // 2, base : base + 8, :] = solve_rest
@@ -365,13 +357,20 @@
     slab = (2, ROWS, LON)
     halo = (5, 2, LON)
     chunks = (DEST, 144, LANES)
-    winds = (tracer, thickness, wind_u, wind_v)
+
+    def transposed(block):
+        return lax.all_to_all(block, "lev", split_axis=0, concat_axis=0, tiled=True)
+
+    fields = [
+        pltpu.with_memory_space_constraint(x, pltpu.HBM)
+        for x in (tracer, thickness, wind_u, wind_v)
+    ]
     to_first, to_second, kept = call(
         edge_kernel,
         [HB] * 4,
-        [(VM, halo), (VM, halo), (VM, (8, 8, LON))],
-        scratch=[pltpu.VMEM((4, 8, LON), f32), pltpu.SemaphoreType.DMA((16,))],
-    )(*[pltpu.with_memory_space_constraint(x, pltpu.HBM) for x in winds])
+        [(VM, halo), (VM, halo), (VM, (7, 8, LON))],
+        scratch=[pltpu.VMEM((4, 2, 4, LON), f32), pltpu.SemaphoreType.DMA((8,))],
+    )(*fields)
     pairs = [[(i, i + 1) for i in range(start, lat_count - 1, 2)] for start in (1, 0)]
     first_halo, second_halo = [
         lax.ppermute(rows, "lat", [p for a, b in pair for p in ((a, b), (b, a))])
@@ -380,32 +379,29 @@
     send, edges = call(
         first_kernel,
         [VM] * 4,
-        [(ANY, chunks), (VM, (2, 8, LON))],
-        scratch=[
-            pltpu.VMEM((4,) + slab, f32),
-            pltpu.VMEM(chunks, f32),
-            pltpu.SemaphoreType.DMA((DEST,)),
-        ],
-    )(*winds)
+        [(VM, chunks), (VM, (2, 8, LON))],
+        scratch=[pltpu.VMEM((2,) + slab, f32)],
+    )(tracer, thickness, wind_u, wind_v)
+    factors = call(
+        factor_kernel,
+        [VM, VM],
+        [(VM, (3, LEVELS, ROWS, LANES)), (VM, (3, LEVELS, 8, LANES))],
+    )(offsets, coupling)
+    edges, *factors = lax.optimization_barrier((edges, *factors))
     (send,) = call(
         second_kernel,
         [VM] * 4 + [ANY],
         [(ANY, chunks)],
         scratch=[
-            pltpu.VMEM((4, 8, LON), f32),
-            pltpu.VMEM(chunks, f32),
-            pltpu.SemaphoreType.DMA((18,)),
+            pltpu.VMEM((2, 8, LON), f32),
+            pltpu.VMEM((DEST, 72, LANES), f32),
+            pltpu.SemaphoreType.DMA((9,)),
         ],
         aliases={4: 0},
     )(first_halo, second_halo, kept, edges, send)
-    received = lax.all_to_all(send, "lev", split_axis=0, concat_axis=0, tiled=True)
-    factors = call(
-        factor_kernel,
-        [VM, VM],
-        [(VM, (3, LEVELS, ROWS, LANES)), (VM, (3, LEVELS, 8, LANES))],
-    )(offsets, coupling)
+    received = transposed(send)
     (back,) = call(column_kernel, [VM] * 3, [(VM, (DEST, 112, LANES))])(received, *factors)
-    returned = lax.all_to_all(back, "lev", split_axis=0, concat_axis=0, tiled=True)
+    returned = transposed(back)
     return tuple(
         call(
             unpack_kernel,

time: 58.4 us -> 57.3 us (0.981)
  blocking collectives: 17.8 us -> 40 us
  waiting for transfers between devices: 19.8 us -> 2.69 us
  starting transfers between devices: 11.1 us -> 6.4 us
  Pallas kernels: 8.67 us -> 7.17 us
    all_to_all x1 -> x2, blocking collectives: 17.8 us -> 40 us  [transposed(): return lax.all_to_all(block, 'lev', split_axis=0, concat_axis=0, tiled=True)]
    all_to_all x1 -> x0, waiting for transfers between devices: 16.3 us -> none  [local(): lax.all_to_all(send, 'lev', split_axis=0, concat_axis=0, tiled=True)]
    all_to_all x1 -> x0, starting transfers between devices: 4.72 us -> none  [local(): lax.all_to_all(send, 'lev', split_axis=0, concat_axis=0, tiled=True)]
    pallas_call x2, Pallas kernels: 4.06 us -> 3.13 us  [the longest x1 1.71 us: local(): call(first_kernel, [VM] * 4, [(VM, chunks), (VM, (2, 8, LON))], scratch=[...]
    ppermute x2, waiting for transfers between devices: 3.48 us -> 2.69 us  [local(): lax.ppermute(rows, 'lat', [p for a, b in pair for p in ((a, b), (b, a))])]
    pallas_call x1, Pallas kernels: 1.42 us -> 0.66 us  [local(): call(second_kernel, [VM] * 4 + [ANY], [(ANY, chunks)], scratch=[pltpu.VME...]
  transfers between devices with their start and end apart: 3 -> 2, of which waited for: 2 -> 1; matrix products, arithmetic and copies ran while one was open for 0% -> 0% of each run, Pallas kernels for 8% -> 6%
where the time goes in v2:
time: 57.3 us; the launch traced here: 57.1 us
  blocking collectives  40 us (70%)
  Pallas kernels  7.17 us (13%)
  starting transfers between devices  6.4 us (11%)
  waiting for transfers between devices  2.69 us (5%)
  between operations  0.78 us (1%)
    all_to_all x2, blocking collectives, transposed(): return lax.all_to_all(block, 'lev', split_axis=0, concat_axis=0, tiled=True)  40 us
    ppermute x2, starting transfers between devices, local(): lax.ppermute(rows, 'lat', [p for a, b in pair for p in ((a, b), (b, a))])  6.4 us
    ppermute x2, waiting for transfers between devices, local(): lax.ppermute(rows, 'lat', [p for a, b in pair for p in ((a, b), (b, a))])  2.69 us
    pallas_call x1, Pallas kernels, local(): call(factor_kernel, [VM, VM], [(VM, (3, LEVELS, ROWS, LANES)), (VM, (3, L...  1.75 us
    pallas_call x1, Pallas kernels, local(): call(first_kernel, [VM] * 4, [(VM, chunks), (VM, (2, 8, LON))], scratch=[...  1.71 us
    pallas_call x1, Pallas kernels, local(): call(edge_kernel, [HB] * 4, [(VM, halo), (VM, halo), (VM, (7, 8, LON))],...  1.42 us
  transfers between devices with their start and end apart: 2, of which 1 were waited for; matrix products, arithmetic and copies ran while one was open for 0% of the time, Pallas kernels for 6%

profile of v2, /device:TPU:70, one launch (start us, length us, event | category | flops | bytes accessed | tf_op | source)
XLA Modules:
  0.0 57.1 jit_solution(12213468986994252661)
XLA Ops:
  0.6 0.0 copy-start.3
  0.6 0.0 copy-start.2
  0.7 0.0 copy-start.1
  0.7 0.0 copy-start
  0.7 0.0 copy-start.5
  0.7 0.0 copy-start.4
  0.7 1.4 %shard_map.85 = (f32[5,2,2304]{2,1,0:T(2,128)S(1)}, f32[5,2,2304]{2,1,0:T(2,128)S(1)}, f32[7,8,2304]{2,1,0:T(8,128)S(1)}) custom-call(f32[2,16,2304]{2,1,0:T(8,128)} %tracer.3, f32[2,16,2304]{2,1,0:T(8,128)} %thickness.3, f32[2,16,2304]{2,1,0:T(8,128)} %wind_u.3, f32[2,16,2304]{2,1,0:T(8,128)} %wind_v.3), custom_call_target="tpu_custom_call" | custom-call | flops 1000000 | bytes 3000000 | tf_op jit(solution)/shard_map/pallas_call | solution.py:368
  2.1 6.3 %collective-permute-start = (f32[5,2,2304]{2,1,0:T(2,128)S(1)}, f32[5,2,2304]{2,1,0:T(2,128)S(1)}, u32[]{:S(2)}, u32[]{:S(2)}) collective-permute-start(f32[5,2,2304]{2,1,0:T(2,128)S(1)} %get-tuple-element.13), channel_id=1, source_target_pairs={{16,32},{32,16},{48,64},{64,48},{80,96},{96,80},{112,128},{128,112... | collective-permute-start | bytes 276488 | tf_op jit(solution)/shard_map/ppermute | solution.py:376
  8.4 0.1 collective-permute-start.1
  8.5 0.0 copy-done.3
  8.5 0.0 copy-done.2
  8.6 0.0 copy-done.1
  8.6 0.0 copy-done
  8.6 1.7 %shard_map.86 = (f32[16,144,128]{2,1,0:T(8,128)S(1)}, f32[2,8,2304]{2,1,0:T(8,128)S(1)}) custom-call(f32[2,16,2304]{2,1,0:T(8,128)S(1)} %copy-done, f32[2,16,2304]{2,1,0:T(8,128)S(1)} %copy-done.1, f32[2,16,2304]{2,1,0:T(8,128)S(1)} %copy-done.2, f32[2,16,2304]{2,1,0:T(8,128)S(1)} %copy-done.3), custom_call_target="tpu_custom_call" | custom-call | flops 1000000 | bytes 3000000 | tf_op jit(solution)/shard_map/pallas_call | solution.py:379
  10.3 0.0 copy-done.5
  10.3 0.0 copy-done.4
  10.3 1.8 %shard_map.87 = (f32[3,32,16,128]{3,2,1,0:T(8,128)S(1)}, f32[3,32,8,128]{3,2,1,0:T(8,128)S(1)}) custom-call(s32[32,16,144]{2,1,0:T(8,128)S(1)} %copy-done.4, f32[31,16,144]{2,1,0:T(8,128)S(1)} %copy-done.5), custom_call_target="tpu_custom_call" | custom-call | flops 1000000 | bytes 3000000 | tf_op jit(solution)/shard_map/pallas_call | solution.py:385
  12.1 2.7 %collective-permute-done.first_halo = f32[5,2,2304]{2,1,0:T(2,128)S(1)} collective-permute-done((f32[5,2,2304]{2,1,0:T(2,128)S(1)}, f32[5,2,2304]{2,1,0:T(2,128)S(1)}, u32[]{:S(2)}, u32[]{:S(2)}) %collective-permute-start) | collective-permute-done | bytes 92192 | tf_op jit(solution)/shard_map/ppermute | solution.py:376
  14.8 0.0 collective-permute-done.1.second_halo
  14.8 0.7 %shard_map.88 = f32[16,144,128]{2,1,0:T(8,128)S(1)} custom-call(f32[5,2,2304]{2,1,0:T(2,128)S(1)} %collective-permute-done.first_halo, f32[5,2,2304]{2,1,0:T(2,128)S(1)} %collective-permute-done.1.second_halo, f32[7,8,2304]{2,1,0:T(8,128)S(1)} %get-tuple-element.15.kept, f32[2,8,2304]{2,1,0:T(8,128)S(1)} %get-tuple-element.19.edges, ...), custom_call_target="tpu_custom_call", output_to_operand_aliasing={{}: (4, {})} | custom-call | flops 1000000 | bytes 3000000 | tf_op jit(solution)/shard_map/pallas_call | solution.py:391
  15.4 22.3 %all_to_all.10.received = f32[16,144,128]{2,1,0:T(8,128)S(1)} all-to-all(f32[16,144,128]{2,1,0:T(8,128)S(1)} %shard_map.88), channel_id=1, replica_groups=mesh['lat'=16,'lev'=16] {'lev'}, dimensions={0} | all-to-all | bytes 2359296 | tf_op jit(solution)/shard_map/all_to_all | solution.py:362
  37.8 0.6 %shard_map.89 = f32[16,112,128]{2,1,0:T(8,128)S(1)} custom-call(f32[16,144,128]{2,1,0:T(8,128)S(1)} %all_to_all.10.received, f32[3,32,16,128]{3,2,1,0:T(8,128)S(1)} %get-tuple-element.21.factors_main, f32[3,32,8,128]{3,2,1,0:T(8,128)S(1)} %get-tuple-element.22.factors_rest), custom_call_target="tpu_custom_call" | custom-call | flops 1000000 | bytes 3000000 | tf_op jit(solution)/shard_map/pallas_call | solution.py:403
  38.3 17.7 %all_to_all.11.received = f32[16,112,128]{2,1,0:T(8,128)S(1)} all-to-all(f32[16,112,128]{2,1,0:T(8,128)S(1)} %shard_map.89), channel_id=1, replica_groups=mesh['lat'=16,'lev'=16] {'lev'}, dimensions={0} | all-to-all | bytes 1835008 | tf_op jit(solution)/shard_map/all_to_all | solution.py:362
  56.0 1.1 %shard_map.90 = (f32[2,16,2304]{2,1,0:T(8,128)}, f32[2,16,2304]{2,1,0:T(8,128)}, f32[2,16,2304]{2,1,0:T(8,128)}) custom-call(f32[16,112,128]{2,1,0:T(8,128)S(1)} %all_to_all.11.received), custom_call_target="tpu_custom_call" | custom-call | flops 1000000 | bytes 3000000 | tf_op jit(solution)/shard_map/pallas_call | solution.py:406
Async XLA Ops:
  0.6 7.9 %copy-start.3 = (f32[2,16,2304]{2,1,0:T(8,128)S(1)}, f32[2,16,2304]{2,1,0:T(8,128)}, u32[]{:S(2)}) copy-start(f32[2,16,2304]{2,1,0:T(8,128)} %wind_v.3) | copy-start | bytes 884740
  0.6 7.9 %copy-start.2 = (f32[2,16,2304]{2,1,0:T(8,128)S(1)}, f32[2,16,2304]{2,1,0:T(8,128)}, u32[]{:S(2)}) copy-start(f32[2,16,2304]{2,1,0:T(8,128)} %wind_u.3) | copy-start | bytes 884740
  0.7 7.9 %copy-start.1 = (f32[2,16,2304]{2,1,0:T(8,128)S(1)}, f32[2,16,2304]{2,1,0:T(8,128)}, u32[]{:S(2)}) copy-start(f32[2,16,2304]{2,1,0:T(8,128)} %thickness.3) | copy-start | bytes 884740
  0.7 7.9 %copy-start = (f32[2,16,2304]{2,1,0:T(8,128)S(1)}, f32[2,16,2304]{2,1,0:T(8,128)}, u32[]{:S(2)}) copy-start(f32[2,16,2304]{2,1,0:T(8,128)} %tracer.3) | copy-start | bytes 884740
  0.7 9.6 %copy-start.5 = (f32[31,16,144]{2,1,0:T(8,128)S(1)}, f32[31,16,144]{2,1,0:T(8,128)}, u32[]{:S(2)}) copy-start(f32[31,16,144]{2,1,0:T(8,128)} %coupling.1) | copy-start | bytes 857092
  0.7 9.6 %copy-start.4 = (s32[32,16,144]{2,1,0:T(8,128)S(1)}, s32[32,16,144]{2,1,0:T(8,128)}, u32[]{:S(2)}) copy-start(s32[32,16,144]{2,1,0:T(8,128)} %offsets.1) | copy-start | bytes 884740
  2.1 12.6 %collective-permute-start = (f32[5,2,2304]{2,1,0:T(2,128)S(1)}, f32[5,2,2304]{2,1,0:T(2,128)S(1)}, u32[]{:S(2)}, u32[]{:S(2)}) collective-permute-start(f32[5,2,2304]{2,1,0:T(2,128)S(1)} %get-tuple-element.13), channel_id=1, source_target_pairs={{16,32},{32,16},{48,64},{64,48},{80,96},{96,80},{112,128},{128,112... | collective-permute-start | bytes 276488 | tf_op jit(solution)/shard_map/ppermute | solution.py:376
  8.4 6.3 %collective-permute-start.1 = (f32[5,2,2304]{2,1,0:T(2,128)S(1)}, f32[5,2,2304]{2,1,0:T(2,128)S(1)}, u32[]{:S(2)}, u32[]{:S(2)}) collective-permute-start(f32[5,2,2304]{2,1,0:T(2,128)S(1)} %get-tuple-element.14), channel_id=1, source_target_pairs={{0,16},{16,0},{32,48},{48,32},{64,80},{80,64},{96,112},{112,96},{1... | collective-permute-start | bytes 276488 | tf_op jit(solution)/shard_map/ppermute | solution.py:376

commit v3 on v2

--- a/solution.py
+++ b/solution.py
@@ -371,10 +371,20 @@
         [(VM, halo), (VM, halo), (VM, (7, 8, LON))],
         scratch=[pltpu.VMEM((4, 2, 4, LON), f32), pltpu.SemaphoreType.DMA((8,))],
     )(*fields)
-    pairs = [[(i, i + 1) for i in range(start, lat_count - 1, 2)] for start in (1, 0)]
+    lev_count = lax.axis_size("lev")
+    moves = []
+    for start in (1, 0):
+        pairs = [(i, i + 1) for i in range(start, lat_count - 1, 2)]
+        lats = dict(pairs + [(b, a) for a, b in pairs])
+        moves.append(
+            [
+                (lat * lev_count + lev, lats[lat] * lev_count + lev if lat in lats else lat * lev_count + (lev ^ 1))
+                for lat in range(lat_count)
+                for lev in range(lev_count)
+            ]
+        )
     first_halo, second_halo = [
-        lax.ppermute(rows, "lat", [p for a, b in pair for p in ((a, b), (b, a))])
-        for rows, pair in zip((to_first, to_second), pairs)
+        lax.ppermute(rows, ("lat", "lev"), move) for rows, move in zip((to_first, to_second), moves)
     ]
     send, edges = call(
         first_kernel,

time: 57.3 us -> 55.5 us (0.969)
  starting transfers between devices: 6.4 us -> 4.49 us
    ppermute x2, starting transfers between devices: 6.4 us -> 4.49 us  [local(): lax.ppermute(rows, ('lat', 'lev'), move)]
where the time goes in v3:
time: 55.5 us; the launch traced here: 55.3 us
  blocking collectives  40 us (72%)
  Pallas kernels  7.17 us (13%)
  starting transfers between devices  4.49 us (8%)
  waiting for transfers between devices  2.82 us (5%)
  between operations  0.76 us (1%)
    all_to_all x2, blocking collectives, transposed(): return lax.all_to_all(block, 'lev', split_axis=0, concat_axis=0, tiled=True)  40 us
    ppermute x2, starting transfers between devices, local(): lax.ppermute(rows, ('lat', 'lev'), move)  4.49 us
    ppermute x2, waiting for transfers between devices, local(): lax.ppermute(rows, ('lat', 'lev'), move)  2.82 us
    pallas_call x1, Pallas kernels, local(): call(factor_kernel, [VM, VM], [(VM, (3, LEVELS, ROWS, LANES)), (VM, (3, L...  1.75 us
    pallas_call x1, Pallas kernels, local(): call(first_kernel, [VM] * 4, [(VM, chunks), (VM, (2, 8, LON))], scratch=[...  1.71 us
    pallas_call x1, Pallas kernels, local(): call(edge_kernel, [HB] * 4, [(VM, halo), (VM, halo), (VM, (7, 8, LON))],...  1.42 us
  transfers between devices with their start and end apart: 2, of which 1 were waited for; matrix products, arithmetic and copies ran while one was open for 0% of the time, Pallas kernels for 6%

profile of v3, /device:TPU:70, one launch (start us, length us, event | category | flops | bytes accessed | tf_op | source)
XLA Modules:
  0.0 55.3 jit_solution(5862425143611043172)
XLA Ops:
  0.6 0.0 copy-start.3
  0.6 0.0 copy-start.2
  0.7 0.0 copy-start.1
  0.7 0.0 copy-start
  0.7 0.0 copy-start.5
  0.7 0.0 copy-start.4
  0.7 1.4 %shard_map.85 = (f32[5,2,2304]{2,1,0:T(2,128)S(1)}, f32[5,2,2304]{2,1,0:T(2,128)S(1)}, f32[7,8,2304]{2,1,0:T(8,128)S(1)}) custom-call(f32[2,16,2304]{2,1,0:T(8,128)} %tracer.3, f32[2,16,2304]{2,1,0:T(8,128)} %thickness.3, f32[2,16,2304]{2,1,0:T(8,128)} %wind_u.3, f32[2,16,2304]{2,1,0:T(8,128)} %wind_v.3), custom_call_target="tpu_custom_call" | custom-call | flops 1000000 | bytes 3000000 | tf_op jit(solution)/shard_map/pallas_call | solution.py:368
  2.1 4.5 %collective-permute-start = (f32[5,2,2304]{2,1,0:T(2,128)S(1)}, f32[5,2,2304]{2,1,0:T(2,128)S(1)}, u32[]{:S(2)}, u32[]{:S(2)}) collective-permute-start(f32[5,2,2304]{2,1,0:T(2,128)S(1)} %get-tuple-element.13), channel_id=1, source_target_pairs={{0,1},{1,0},{2,3},{3,2},{4,5},{5,4},{6,7},{7,6},{8,9},{9,8},{10,11... | collective-permute-start | bytes 276488 | tf_op jit(solution)/shard_map/ppermute | solution.py:387
  6.6 0.0 collective-permute-start.1
  6.6 0.0 copy-done.3
  6.6 0.0 copy-done.2
  6.6 0.0 copy-done.1
  6.6 0.0 copy-done
  6.6 1.7 %shard_map.86 = (f32[16,144,128]{2,1,0:T(8,128)S(1)}, f32[2,8,2304]{2,1,0:T(8,128)S(1)}) custom-call(f32[2,16,2304]{2,1,0:T(8,128)S(1)} %copy-done, f32[2,16,2304]{2,1,0:T(8,128)S(1)} %copy-done.1, f32[2,16,2304]{2,1,0:T(8,128)S(1)} %copy-done.2, f32[2,16,2304]{2,1,0:T(8,128)S(1)} %copy-done.3), custom_call_target="tpu_custom_call" | custom-call | flops 1000000 | bytes 3000000 | tf_op jit(solution)/shard_map/pallas_call | solution.py:389
  8.4 0.0 copy-done.5
  8.4 0.0 copy-done.4
  8.4 1.8 %shard_map.87 = (f32[3,32,16,128]{3,2,1,0:T(8,128)S(1)}, f32[3,32,8,128]{3,2,1,0:T(8,128)S(1)}) custom-call(s32[32,16,144]{2,1,0:T(8,128)S(1)} %copy-done.4, f32[31,16,144]{2,1,0:T(8,128)S(1)} %copy-done.5), custom_call_target="tpu_custom_call" | custom-call | flops 1000000 | bytes 3000000 | tf_op jit(solution)/shard_map/pallas_call | solution.py:395
  10.1 2.8 %collective-permute-done.first_halo = f32[5,2,2304]{2,1,0:T(2,128)S(1)} collective-permute-done((f32[5,2,2304]{2,1,0:T(2,128)S(1)}, f32[5,2,2304]{2,1,0:T(2,128)S(1)}, u32[]{:S(2)}, u32[]{:S(2)}) %collective-permute-start) | collective-permute-done | bytes 92192 | tf_op jit(solution)/shard_map/ppermute | solution.py:387
  13.0 0.0 collective-permute-done.1.second_halo
  13.0 0.7 %shard_map.88 = f32[16,144,128]{2,1,0:T(8,128)S(1)} custom-call(f32[5,2,2304]{2,1,0:T(2,128)S(1)} %collective-permute-done.first_halo, f32[5,2,2304]{2,1,0:T(2,128)S(1)} %collective-permute-done.1.second_halo, f32[7,8,2304]{2,1,0:T(8,128)S(1)} %get-tuple-element.15.kept, f32[2,8,2304]{2,1,0:T(8,128)S(1)} %get-tuple-element.19.edges, ...), custom_call_target="tpu_custom_call", output_to_operand_aliasing={{}: (4, {})} | custom-call | flops 1000000 | bytes 3000000 | tf_op jit(solution)/shard_map/pallas_call | solution.py:401
  13.6 22.3 %all_to_all.10.received = f32[16,144,128]{2,1,0:T(8,128)S(1)} all-to-all(f32[16,144,128]{2,1,0:T(8,128)S(1)} %shard_map.88), channel_id=1, replica_groups=mesh['lat'=16,'lev'=16] {'lev'}, dimensions={0} | all-to-all | bytes 2359296 | tf_op jit(solution)/shard_map/all_to_all | solution.py:362
  36.0 0.6 %shard_map.89 = f32[16,112,128]{2,1,0:T(8,128)S(1)} custom-call(f32[16,144,128]{2,1,0:T(8,128)S(1)} %all_to_all.10.received, f32[3,32,16,128]{3,2,1,0:T(8,128)S(1)} %get-tuple-element.21.factors_main, f32[3,32,8,128]{3,2,1,0:T(8,128)S(1)} %get-tuple-element.22.factors_rest), custom_call_target="tpu_custom_call" | custom-call | flops 1000000 | bytes 3000000 | tf_op jit(solution)/shard_map/pallas_call | solution.py:413
  36.5 17.7 %all_to_all.11.received = f32[16,112,128]{2,1,0:T(8,128)S(1)} all-to-all(f32[16,112,128]{2,1,0:T(8,128)S(1)} %shard_map.89), channel_id=1, replica_groups=mesh['lat'=16,'lev'=16] {'lev'}, dimensions={0} | all-to-all | bytes 1835008 | tf_op jit(solution)/shard_map/all_to_all | solution.py:362
  54.2 1.1 %shard_map.90 = (f32[2,16,2304]{2,1,0:T(8,128)}, f32[2,16,2304]{2,1,0:T(8,128)}, f32[2,16,2304]{2,1,0:T(8,128)}) custom-call(f32[16,112,128]{2,1,0:T(8,128)S(1)} %all_to_all.11.received), custom_call_target="tpu_custom_call" | custom-call | flops 1000000 | bytes 3000000 | tf_op jit(solution)/shard_map/pallas_call | solution.py:416
Async XLA Ops:
  0.6 6.0 %copy-start.3 = (f32[2,16,2304]{2,1,0:T(8,128)S(1)}, f32[2,16,2304]{2,1,0:T(8,128)}, u32[]{:S(2)}) copy-start(f32[2,16,2304]{2,1,0:T(8,128)} %wind_v.3) | copy-start | bytes 884740
  0.6 6.0 %copy-start.2 = (f32[2,16,2304]{2,1,0:T(8,128)S(1)}, f32[2,16,2304]{2,1,0:T(8,128)}, u32[]{:S(2)}) copy-start(f32[2,16,2304]{2,1,0:T(8,128)} %wind_u.3) | copy-start | bytes 884740
  0.7 6.0 %copy-start.1 = (f32[2,16,2304]{2,1,0:T(8,128)S(1)}, f32[2,16,2304]{2,1,0:T(8,128)}, u32[]{:S(2)}) copy-start(f32[2,16,2304]{2,1,0:T(8,128)} %thickness.3) | copy-start | bytes 884740
  0.7 6.0 %copy-start = (f32[2,16,2304]{2,1,0:T(8,128)S(1)}, f32[2,16,2304]{2,1,0:T(8,128)}, u32[]{:S(2)}) copy-start(f32[2,16,2304]{2,1,0:T(8,128)} %tracer.3) | copy-start | bytes 884740
  0.7 7.7 %copy-start.5 = (f32[31,16,144]{2,1,0:T(8,128)S(1)}, f32[31,16,144]{2,1,0:T(8,128)}, u32[]{:S(2)}) copy-start(f32[31,16,144]{2,1,0:T(8,128)} %coupling.1) | copy-start | bytes 857092
  0.7 7.7 %copy-start.4 = (s32[32,16,144]{2,1,0:T(8,128)S(1)}, s32[32,16,144]{2,1,0:T(8,128)}, u32[]{:S(2)}) copy-start(s32[32,16,144]{2,1,0:T(8,128)} %offsets.1) | copy-start | bytes 884740
  2.1 10.8 %collective-permute-start = (f32[5,2,2304]{2,1,0:T(2,128)S(1)}, f32[5,2,2304]{2,1,0:T(2,128)S(1)}, u32[]{:S(2)}, u32[]{:S(2)}) collective-permute-start(f32[5,2,2304]{2,1,0:T(2,128)S(1)} %get-tuple-element.13), channel_id=1, source_target_pairs={{0,1},{1,0},{2,3},{3,2},{4,5},{5,4},{6,7},{7,6},{8,9},{9,8},{10,11... | collective-permute-start | bytes 276488 | tf_op jit(solution)/shard_map/ppermute | solution.py:387
  6.6 6.4 %collective-permute-start.1 = (f32[5,2,2304]{2,1,0:T(2,128)S(1)}, f32[5,2,2304]{2,1,0:T(2,128)S(1)}, u32[]{:S(2)}, u32[]{:S(2)}) collective-permute-start(f32[5,2,2304]{2,1,0:T(2,128)S(1)} %get-tuple-element.14), channel_id=1, source_target_pairs={{0,16},{1,17},{2,18},{3,19},{4,20},{5,21},{6,22},{7,23},{8,24},{9,... | collective-permute-start | bytes 276488 | tf_op jit(solution)/shard_map/ppermute | solution.py:387

commit v4 on v3

--- a/solution.py
+++ b/solution.py
@@ -62,7 +62,11 @@
     for copy in copies:
         copy.wait()
     tracer, layer, u, v = [
-        jnp.concatenate([fetched[slot, 0], fetched[slot, 1]], axis=0) for slot in range(4)
+        jnp.concatenate(
+            [fetched[slot, 0, 0:2], fetched[slot, 1, 2:4], fetched[slot, 1, 0:2], fetched[slot, 0, 2:4]],
+            axis=0,
+        )
+        for slot in range(4)
     ]
     mass = tracer * layer
     east = courant(east_roll(u) + u)
@@ -81,32 +85,13 @@
     for slot, value in enumerate(values):
         for level in range(2):
             south = value[4 * level : 4 * level + 1]
-            north_row = value[4 * level + 3 : 4 * level + 4]
+            north_row = value[7 - 4 * level : 8 - 4 * level]
             to_first[slot, level : level + 1, :] = jnp.where(north_first, north_row, south)
             to_second[slot, level : level + 1, :] = jnp.where(north_first, south, north_row)
         kept[slot] = value
     kept[5] = east
     kept[6] = jnp.where(upper, jnp.minimum(inner, 0.0), -jnp.maximum(inner, 0.0))
-
-
-def pack_pair(load, store, places):
-    lane = lane_ids(ROWS)
-    lane8 = lane_ids(8)
-    for dest in range(DEST):
-        tile = dest + dest // 8
-        shift = 16 * (dest % 8)
-        packed = None
-        for place, field, level in places:
-            here, after = load(field, level, tile), load(field, level, tile + 1)
-            block = here if shift == 0 else jnp.where(lane >= shift, here, after)
-            store(dest, (field * 2 + level) * ROWS, block)
-            for half in range(2):
-                part = after[8 * half : 8 * half + 8]
-                part = pltpu.roll(part, 2, 0) if half else part
-                start = place + 16 * half
-                part = pltpu.roll(part, (start - shift) % LANES, 1)
-                packed = part if packed is None else jnp.where(lane8 >= start, part, packed)
-        store(dest, 64, packed)
+    kept[7] = u
 
 
 def first_kernel(tracer, thickness, wind_u, wind_v, send, edges, held):
@@ -116,32 +101,43 @@
         mass = tracer[level] * layer
         east = courant(east_roll(u) + u)
         north = jnp.where(row == 0, 0.0, courant(pltpu.roll(v, 1, 0) + v))
+        done = []
         for slot, m in enumerate((mass, layer)):
             for substep in range(2):
                 flux = upwind(north, pltpu.roll(m, 1, 0), m)
                 above = jnp.where(row == ROWS - 1, 0.0, pltpu.roll(flux, ROWS - 1, 0))
                 m = m + zonal(east, m) + flux - above
             edges[slot, 4 * level : 4 * level + 2, :] = m[0:2]
-            edges[slot, 4 * level + 2 : 4 * level + 4, :] = m[14:16]
-            held[slot, level] = m
-
-    def load(field, level, tile):
-        return held[field, level, :, tile * LANES : (tile + 1) * LANES]
-
-    def load_wind(field, level, tile):
-        return (wind_u, wind_v)[field][level, :, tile * LANES : (tile + 1) * LANES]
-
-    def store(dest, row, value):
-        send[dest, row : row + value.shape[0], :] = value
-
-    def store_wind(dest, row, value):
-        store(dest, 72 + row, value)
-
-    pack_pair(load, store, ((0, 0, 0), (32, 1, 0), (64, 0, 1), (96, 1, 1)))
-    pack_pair(load_wind, store_wind, ((0, 1, 1), (32, 0, 0), (64, 1, 0), (96, 0, 1)))
-
-
-def second_kernel(first_halo, second_halo, kept, edges, sent, send, held, patch, sems):
+            edges[slot, 6 - 4 * level : 8 - 4 * level, :] = m[14:16]
+            done.append(m)
+        mass, layer = done
+        for field, m in enumerate((mass, layer * u, layer * v, layer)):
+            held[field, level] = m
+    lane = lane_ids(ROWS)
+    lane8 = lane_ids(8)
+    for dest in range(DEST):
+        tile = dest + dest // 8
+        shift = 16 * (dest % 8)
+        low = slice(tile * LANES, (tile + 1) * LANES)
+        high = slice((tile + 1) * LANES, (tile + 2) * LANES)
+        for level in range(2):
+            packed = None
+            for field in range(4):
+                here = held[field, level, :, low]
+                after = held[field, level, :, high]
+                block = here if shift == 0 else jnp.where(lane >= shift, here, after)
+                start = (field * 2 + level) * ROWS
+                send[dest, start : start + ROWS, :] = block
+                for half in range(2):
+                    part = after[8 * half : 8 * half + 8]
+                    part = pltpu.roll(part, 2, 0) if half else part
+                    place = 32 * field + 16 * half
+                    part = pltpu.roll(part, (place - shift) % LANES, 1)
+                    packed = part if packed is None else jnp.where(lane8 >= place, part, packed)
+            send[dest, 128 + 8 * level : 136 + 8 * level, :] = packed
+
+
+def second_kernel(first_halo, second_halo, kept, edges, sent, send, held):
     lat = lax.axis_index("lat")
     row = lax.rem(row_ids(8), 4)
     upper = row >= 2
@@ -152,18 +148,19 @@
     open_face = jnp.where(upper, north_open, south_open)
 
     def halo(slot):
-        rows = []
+        south, north = [], []
         for level in range(2):
             one = first_halo[slot, level : level + 1, :]
             two = second_halo[slot, level : level + 1, :]
-            south = jnp.where(even, one, two)
-            north = jnp.where(even, two, one)
-            rows.append(jnp.where(upper[0:4], north, south))
+            south.append(jnp.where(even, one, two))
+            north.append(jnp.where(even, two, one))
+        rows = [jnp.where(upper[0:4], north[1 - level], south[level]) for level in range(2)]
         return jnp.concatenate(rows, axis=0)
 
     v, east, inner = kept[0], kept[5], kept[6]
     flow = open_face * courant(v + halo(0))
     sign = jnp.where(upper, -1.0, 1.0)
+    done = []
     for slot in range(2):
         m, m_beyond = kept[1 + slot], halo(1 + slot)
         partial, beyond = kept[3 + slot], halo(3 + slot)
@@ -175,38 +172,43 @@
         carried = inner * change
         gain = change + zonal(east, change) + carried + sign * flux
         passed = jnp.where(row == 1, pltpu.roll(carried, 1, 0), pltpu.roll(carried, 7, 0))
-        held[slot] = edges[slot] + jnp.where(outer, gain, -passed)
+        done.append(edges[slot] + jnp.where(outer, gain, -passed))
+    mass, layer = done
+    for field, m in enumerate((mass, layer * kept[7], layer * v, layer)):
+        held[field] = m
     lane = lane_ids(8)
+    upper_half = lax.rem(lane, 32) >= 16
+    place = lax.broadcasted_iota(jnp.int32, (8, LANES), 0)
+    low_ends, high_ends = place < 2, place >= 6
     for dest in range(DEST):
         tile = dest + dest // 8
         shift = 16 * (dest % 8)
         low = slice(tile * LANES, (tile + 1) * LANES)
         high = slice((tile + 1) * LANES, (tile + 2) * LANES)
-        packed = None
-        for level in range(2):
-            for field in range(2):
-                here, after = held[field, :, low], held[field, :, high]
-                block = here if shift == 0 else jnp.where(lane >= shift, here, after)
+        halves = [None, None]
+        for field in range(4):
+            here, after = held[field, :, low], held[field, :, high]
+            block = here if shift == 0 else jnp.where(lane >= shift, here, after)
+            for level in range(2):
+                ends = pltpu.roll(block, 4, 0) if level else block
                 start = (field * 2 + level) * ROWS
-                patch[dest, start : start + 2, :] = block[4 * level : 4 * level + 2]
-                patch[dest, start + 14 : start + 16, :] = block[4 * level + 2 : 4 * level + 4]
-                for half in range(2):
-                    start = 64 * level + 32 * field + 16 * half
-                    part = pltpu.roll(after, (8 - 4 * level - 2 * half) % 8, 0)
-                    part = pltpu.roll(part, (start - shift) % LANES, 1)
-                    packed = part if packed is None else jnp.where(lane >= start, part, packed)
-        patch[dest, 64:66, :] = packed[0:2]
-    spots = [16 * i + end for i in range(4) for end in (0, 14)] + [64]
-    copies = [
-        pltpu.make_async_copy(
-            patch.at[:, pl.ds(spot, 2), :], send.at[:, pl.ds(spot, 2), :], sems.at[i]
-        )
-        for i, spot in enumerate(spots)
-    ]
-    for copy in copies:
-        copy.start()
-    for copy in copies:
-        copy.wait()
+                rows = sent[dest, start : start + 8, :]
+                send[dest, start : start + 8, :] = jnp.where(low_ends, ends, rows)
+                rows = sent[dest, start + 8 : start + 16, :]
+                send[dest, start + 8 : start + 16, :] = jnp.where(high_ends, ends, rows)
+            for half in range(2):
+                part = pltpu.roll(after, (32 * field + 16 * half - shift) % LANES, 1)
+                halves[half] = jnp.where(lane >= 32 * field, part, halves[half]) if field else part
+        first, last = halves
+        for level, ends in enumerate(
+            (
+                jnp.where(upper_half, pltpu.roll(last, 2, 0), first),
+                jnp.where(upper_half, pltpu.roll(last, 6, 0), pltpu.roll(first, 4, 0)),
+            )
+        ):
+            start = 128 + 8 * level
+            rows = sent[dest, start : start + 8, :]
+            send[dest, start : start + 8, :] = jnp.where(low_ends, ends, rows)
 
 
 def factor_kernel(offsets, coupling, factors_main, factors_rest):
@@ -240,21 +242,15 @@
 
 
 def column_kernel(received, factors_main, factors_rest, send):
-    group = lane_ids(8) // 32
+    lane = lane_ids(8)
 
     def main(k):
         base = (k % 2) * ROWS
-        mass, layer = [received[k // 2, base + 32 * f : base + 32 * f + ROWS, :] for f in range(2)]
-        u, v = [received[k // 2, base + 72 + 32 * f : base + 72 + 32 * f + ROWS, :] for f in range(2)]
-        return [mass, layer * u, layer * v, layer]
+        return [received[k // 2, base + 32 * f : base + 32 * f + ROWS, :] for f in range(4)]
 
     def rest(k):
-        mass, wind = received[k // 2, 64:72, :], received[k // 2, 136:144, :]
-        if k % 2:
-            mass, wind = pltpu.roll(mass, 64, 1), pltpu.roll(wind, 64, 1)
-        layer = jnp.where(group == 0, pltpu.roll(mass, 96, 1), mass)
-        layer = jnp.where(group >= 2, pltpu.roll(layer, 64, 1), layer)
-        return [jnp.where(group == 0, mass, layer * wind), layer]
+        base = 128 + 8 * (k % 2)
+        return received[k // 2, base : base + 8, :]
 
     def picked(below, above, sums):
         return jnp.where(below, sums[0], jnp.where(above, sums[2], sums[1]))
@@ -268,7 +264,7 @@
         nonlocal main_here, rest_here
         main_next, rest_next = main(k + 1), rest(k + 1)
         main_sums.append([a + b for a, b in zip(main_here, main_next)])
-        rest_sums.append([a + b for a, b in zip(rest_here, rest_next)])
+        rest_sums.append(rest_here + rest_next)
         main_here, rest_here = main_next, rest_next
 
     push(0)
@@ -287,7 +283,9 @@
             send[k // 2, base : base + ROWS, :] = solve_main[f]
         scale = factors_rest[0, k]
         below, above = scale < 0.0, factors_rest[2, k] < 0.0
-        value, total = [picked(below, above, [rest_sums[i][f] for i in three]) for f in range(2)]
+        value = picked(below, above, [rest_sums[i] for i in three])
+        total = jnp.where(lane >= 64, pltpu.roll(value, 96, 1), pltpu.roll(value, 32, 1))
+        total = jnp.where(lane >= 32, jnp.where(lane >= 64, total, pltpu.roll(value, 64, 1)), total)
         solve_rest = value * (jnp.abs(scale) / total) + factors_rest[1, k] * solve_rest
         base = 96 + 8 * (k % 2)
         send[k // 2, base : base + 8, :] = solve_rest
@@ -368,7 +366,7 @@
     to_first, to_second, kept = call(
         edge_kernel,
         [HB] * 4,
-        [(VM, halo), (VM, halo), (VM, (7, 8, LON))],
+        [(VM, halo), (VM, halo), (VM, (8, 8, LON))],
         scratch=[pltpu.VMEM((4, 2, 4, LON), f32), pltpu.SemaphoreType.DMA((8,))],
     )(*fields)
     lev_count = lax.axis_size("lev")
@@ -390,7 +388,7 @@
         first_kernel,
         [VM] * 4,
         [(VM, chunks), (VM, (2, 8, LON))],
-        scratch=[pltpu.VMEM((2,) + slab, f32)],
+        scratch=[pltpu.VMEM((4,) + slab, f32)],
     )(tracer, thickness, wind_u, wind_v)
     factors = call(
         factor_kernel,
@@ -400,14 +398,9 @@
     edges, *factors = lax.optimization_barrier((edges, *factors))
     (send,) = call(
         second_kernel,
-        [VM] * 4 + [ANY],
-        [(ANY, chunks)],
-        scratch=[
-            pltpu.VMEM((2, 8, LON), f32),
-            pltpu.VMEM((DEST, 72, LANES), f32),
-            pltpu.SemaphoreType.DMA((9,)),
-        ],
-        aliases={4: 0},
+        [VM] * 5,
+        [(VM, chunks)],
+        scratch=[pltpu.VMEM((4, 8, LON), f32)],
     )(first_halo, second_halo, kept, edges, send)
     received = transposed(send)
     (back,) = call(column_kernel, [VM] * 3, [(VM, (DEST, 112, LANES))])(received, *factors)

time: 55.5 us -> 55.2 us (level)
  no operation moved by 1% of the time
where the time goes in v4:
time: 55.2 us; the launch traced here: 55 us
  blocking collectives  40 us (72%)
  Pallas kernels  6.89 us (12%)
  starting transfers between devices  4.49 us (8%)
  waiting for transfers between devices  2.8 us (5%)
  between operations  0.76 us (1%)
    all_to_all x2, blocking collectives, transposed(): return lax.all_to_all(block, 'lev', split_axis=0, concat_axis=0, tiled=True)  40 us
    ppermute x2, starting transfers between devices, local(): lax.ppermute(rows, ('lat', 'lev'), move)  4.49 us
    ppermute x2, waiting for transfers between devices, local(): lax.ppermute(rows, ('lat', 'lev'), move)  2.8 us
    pallas_call x1, Pallas kernels, local(): call(factor_kernel, [VM, VM], [(VM, (3, LEVELS, ROWS, LANES)), (VM, (3, L...  1.75 us
    pallas_call x1, Pallas kernels, local(): call(first_kernel, [VM] * 4, [(VM, chunks), (VM, (2, 8, LON))], scratch=[...  1.73 us
    pallas_call x1, Pallas kernels, local(): call(edge_kernel, [HB] * 4, [(VM, halo), (VM, halo), (VM, (8, 8, LON))],...  1.45 us
  transfers between devices with their start and end apart: 2, of which 1 were waited for; matrix products, arithmetic and copies ran while one was open for 0% of the time, Pallas kernels for 6%

profile of v4, /device:TPU:70, one launch (start us, length us, event | category | flops | bytes accessed | tf_op | source)
XLA Modules:
  0.0 55.0 jit_solution(2485286105633303564)
XLA Ops:
  0.6 0.0 copy-start.3
  0.6 0.0 copy-start.2
  0.7 0.0 copy-start.1
  0.7 0.0 copy-start
  0.7 0.0 copy-start.5
  0.7 0.0 copy-start.4
  0.7 1.4 %shard_map.85 = (f32[5,2,2304]{2,1,0:T(2,128)S(1)}, f32[5,2,2304]{2,1,0:T(2,128)S(1)}, f32[8,8,2304]{2,1,0:T(8,128)S(1)}) custom-call(f32[2,16,2304]{2,1,0:T(8,128)} %tracer.3, f32[2,16,2304]{2,1,0:T(8,128)} %thickness.3, f32[2,16,2304]{2,1,0:T(8,128)} %wind_u.3, f32[2,16,2304]{2,1,0:T(8,128)} %wind_v.3), custom_call_target="tpu_custom_call" | custom-call | flops 1000000 | bytes 3000000 | tf_op jit(solution)/shard_map/pallas_call | solution.py:366
  2.1 4.5 %collective-permute-start = (f32[5,2,2304]{2,1,0:T(2,128)S(1)}, f32[5,2,2304]{2,1,0:T(2,128)S(1)}, u32[]{:S(2)}, u32[]{:S(2)}) collective-permute-start(f32[5,2,2304]{2,1,0:T(2,128)S(1)} %get-tuple-element.13), channel_id=1, source_target_pairs={{0,1},{1,0},{2,3},{3,2},{4,5},{5,4},{6,7},{7,6},{8,9},{9,8},{10,11... | collective-permute-start | bytes 276488 | tf_op jit(solution)/shard_map/ppermute | solution.py:385
  6.6 0.0 collective-permute-start.1
  6.6 0.0 copy-done.3
  6.6 0.0 copy-done.2
  6.6 0.0 copy-done.1
  6.7 0.0 copy-done
  6.7 1.7 %shard_map.86 = (f32[16,144,128]{2,1,0:T(8,128)S(1)}, f32[2,8,2304]{2,1,0:T(8,128)S(1)}) custom-call(f32[2,16,2304]{2,1,0:T(8,128)S(1)} %copy-done, f32[2,16,2304]{2,1,0:T(8,128)S(1)} %copy-done.1, f32[2,16,2304]{2,1,0:T(8,128)S(1)} %copy-done.2, f32[2,16,2304]{2,1,0:T(8,128)S(1)} %copy-done.3), custom_call_target="tpu_custom_call" | custom-call | flops 1000000 | bytes 3000000 | tf_op jit(solution)/shard_map/pallas_call | solution.py:387
  8.4 0.0 copy-done.5
  8.4 0.0 copy-done.4
  8.4 1.8 %shard_map.87 = (f32[3,32,16,128]{3,2,1,0:T(8,128)S(1)}, f32[3,32,8,128]{3,2,1,0:T(8,128)S(1)}) custom-call(s32[32,16,144]{2,1,0:T(8,128)S(1)} %copy-done.4, f32[31,16,144]{2,1,0:T(8,128)S(1)} %copy-done.5), custom_call_target="tpu_custom_call" | custom-call | flops 1000000 | bytes 3000000 | tf_op jit(solution)/shard_map/pallas_call | solution.py:393
  10.2 2.8 %collective-permute-done.first_halo = f32[5,2,2304]{2,1,0:T(2,128)S(1)} collective-permute-done((f32[5,2,2304]{2,1,0:T(2,128)S(1)}, f32[5,2,2304]{2,1,0:T(2,128)S(1)}, u32[]{:S(2)}, u32[]{:S(2)}) %collective-permute-start) | collective-permute-done | bytes 92192 | tf_op jit(solution)/shard_map/ppermute | solution.py:385
  13.0 0.0 collective-permute-done.1.second_halo
  13.0 0.5 shard_map.88
  13.5 22.3 %all_to_all.10.received = f32[16,144,128]{2,1,0:T(8,128)S(1)} all-to-all(f32[16,144,128]{2,1,0:T(8,128)S(1)} %shard_map.88), channel_id=1, replica_groups=mesh['lat'=16,'lev'=16] {'lev'}, dimensions={0} | all-to-all | bytes 2359296 | tf_op jit(solution)/shard_map/all_to_all | solution.py:360
  35.9 0.4 shard_map.89
  36.2 17.7 %all_to_all.11.received = f32[16,112,128]{2,1,0:T(8,128)S(1)} all-to-all(f32[16,112,128]{2,1,0:T(8,128)S(1)} %shard_map.89), channel_id=1, replica_groups=mesh['lat'=16,'lev'=16] {'lev'}, dimensions={0} | all-to-all | bytes 1835008 | tf_op jit(solution)/shard_map/all_to_all | solution.py:360
  53.9 1.1 %shard_map.90 = (f32[2,16,2304]{2,1,0:T(8,128)}, f32[2,16,2304]{2,1,0:T(8,128)}, f32[2,16,2304]{2,1,0:T(8,128)}) custom-call(f32[16,112,128]{2,1,0:T(8,128)S(1)} %all_to_all.11.received), custom_call_target="tpu_custom_call" | custom-call | flops 1000000 | bytes 3000000 | tf_op jit(solution)/shard_map/pallas_call | solution.py:409
Async XLA Ops:
  0.6 6.0 %copy-start.3 = (f32[2,16,2304]{2,1,0:T(8,128)S(1)}, f32[2,16,2304]{2,1,0:T(8,128)}, u32[]{:S(2)}) copy-start(f32[2,16,2304]{2,1,0:T(8,128)} %wind_v.3) | copy-start | bytes 884740
  0.6 6.0 %copy-start.2 = (f32[2,16,2304]{2,1,0:T(8,128)S(1)}, f32[2,16,2304]{2,1,0:T(8,128)}, u32[]{:S(2)}) copy-start(f32[2,16,2304]{2,1,0:T(8,128)} %wind_u.3) | copy-start | bytes 884740
  0.7 6.0 %copy-start.1 = (f32[2,16,2304]{2,1,0:T(8,128)S(1)}, f32[2,16,2304]{2,1,0:T(8,128)}, u32[]{:S(2)}) copy-start(f32[2,16,2304]{2,1,0:T(8,128)} %thickness.3) | copy-start | bytes 884740
  0.7 6.0 %copy-start = (f32[2,16,2304]{2,1,0:T(8,128)S(1)}, f32[2,16,2304]{2,1,0:T(8,128)}, u32[]{:S(2)}) copy-start(f32[2,16,2304]{2,1,0:T(8,128)} %tracer.3) | copy-start | bytes 884740
  0.7 7.7 %copy-start.5 = (f32[31,16,144]{2,1,0:T(8,128)S(1)}, f32[31,16,144]{2,1,0:T(8,128)}, u32[]{:S(2)}) copy-start(f32[31,16,144]{2,1,0:T(8,128)} %coupling.1) | copy-start | bytes 857092
  0.7 7.7 %copy-start.4 = (s32[32,16,144]{2,1,0:T(8,128)S(1)}, s32[32,16,144]{2,1,0:T(8,128)}, u32[]{:S(2)}) copy-start(s32[32,16,144]{2,1,0:T(8,128)} %offsets.1) | copy-start | bytes 884740
  2.1 10.8 %collective-permute-start = (f32[5,2,2304]{2,1,0:T(2,128)S(1)}, f32[5,2,2304]{2,1,0:T(2,128)S(1)}, u32[]{:S(2)}, u32[]{:S(2)}) collective-permute-start(f32[5,2,2304]{2,1,0:T(2,128)S(1)} %get-tuple-element.13), channel_id=1, source_target_pairs={{0,1},{1,0},{2,3},{3,2},{4,5},{5,4},{6,7},{7,6},{8,9},{9,8},{10,11... | collective-permute-start | bytes 276488 | tf_op jit(solution)/shard_map/ppermute | solution.py:385
  6.6 6.4 %collective-permute-start.1 = (f32[5,2,2304]{2,1,0:T(2,128)S(1)}, f32[5,2,2304]{2,1,0:T(2,128)S(1)}, u32[]{:S(2)}, u32[]{:S(2)}) collective-permute-start(f32[5,2,2304]{2,1,0:T(2,128)S(1)} %get-tuple-element.14), channel_id=1, source_target_pairs={{0,16},{1,17},{2,18},{3,19},{4,20},{5,21},{6,22},{7,23},{8,24},{9,... | collective-permute-start | bytes 276488 | tf_op jit(solution)/shard_map/ppermute | solution.py:385

commit v5 on v4

--- a/solution.py
+++ b/solution.py
@@ -47,7 +47,7 @@
     return flux - west_roll(flux)
 
 
-def edge_kernel(tracer, thickness, wind_u, wind_v, to_first, to_second, kept, fetched, sems):
+def edge_kernel(tracer, thickness, wind_u, wind_v, to_first, to_second, fetched, sems):
     copies = [
         pltpu.make_async_copy(
             ref.at[:, pl.ds(14 * end, 2), :],
@@ -72,8 +72,6 @@
     east = courant(east_roll(u) + u)
     north = courant(v + pltpu.roll(v, 7, 0))
     odd = lax.rem(row_ids(8), 2) == 1
-    upper = lax.rem(row_ids(8), 4) >= 2
-    inner = jnp.where(odd, pltpu.roll(north, 1, 0), north)
 
     def partial(m):
         flux = upwind(north, m, pltpu.roll(m, 7, 0))
@@ -88,27 +86,37 @@
             north_row = value[7 - 4 * level : 8 - 4 * level]
             to_first[slot, level : level + 1, :] = jnp.where(north_first, north_row, south)
             to_second[slot, level : level + 1, :] = jnp.where(north_first, south, north_row)
-        kept[slot] = value
-    kept[5] = east
-    kept[6] = jnp.where(upper, jnp.minimum(inner, 0.0), -jnp.maximum(inner, 0.0))
-    kept[7] = u
-
-
-def first_kernel(tracer, thickness, wind_u, wind_v, send, edges, held):
+
+
+def first_kernel(tracer, thickness, wind_u, wind_v, send, kept, edges, held):
     row = row_ids(ROWS)
     for level in range(2):
         u, v, layer = wind_u[level], wind_v[level], thickness[level]
         mass = tracer[level] * layer
         east = courant(east_roll(u) + u)
         north = jnp.where(row == 0, 0.0, courant(pltpu.roll(v, 1, 0) + v))
+        low, high = slice(4 * level, 4 * level + 2), slice(6 - 4 * level, 8 - 4 * level)
+
+        def keep(slot, value):
+            kept[slot, low, :] = value[0:2]
+            kept[slot, high, :] = value[14:16]
+
+        keep(0, v)
+        keep(5, east)
+        keep(7, u)
+        kept[6, low, :] = jnp.broadcast_to(-jnp.maximum(north[1:2], 0.0), (2, LON))
+        kept[6, high, :] = jnp.broadcast_to(jnp.minimum(north[15:16], 0.0), (2, LON))
         done = []
         for slot, m in enumerate((mass, layer)):
+            keep(1 + slot, m)
             for substep in range(2):
                 flux = upwind(north, pltpu.roll(m, 1, 0), m)
                 above = jnp.where(row == ROWS - 1, 0.0, pltpu.roll(flux, ROWS - 1, 0))
                 m = m + zonal(east, m) + flux - above
-            edges[slot, 4 * level : 4 * level + 2, :] = m[0:2]
-            edges[slot, 6 - 4 * level : 8 - 4 * level, :] = m[14:16]
+                if substep == 0:
+                    keep(3 + slot, m)
+            edges[slot, low, :] = m[0:2]
+            edges[slot, high, :] = m[14:16]
             done.append(m)
         mass, layer = done
         for field, m in enumerate((mass, layer * u, layer * v, layer)):
@@ -363,10 +371,10 @@
         pltpu.with_memory_space_constraint(x, pltpu.HBM)
         for x in (tracer, thickness, wind_u, wind_v)
     ]
-    to_first, to_second, kept = call(
+    to_first, to_second = call(
         edge_kernel,
         [HB] * 4,
-        [(VM, halo), (VM, halo), (VM, (8, 8, LON))],
+        [(VM, halo), (VM, halo)],
         scratch=[pltpu.VMEM((4, 2, 4, LON), f32), pltpu.SemaphoreType.DMA((8,))],
     )(*fields)
     lev_count = lax.axis_size("lev")
@@ -384,10 +392,10 @@
     first_halo, second_halo = [
         lax.ppermute(rows, ("lat", "lev"), move) for rows, move in zip((to_first, to_second), moves)
     ]
-    send, edges = call(
+    send, kept, edges = call(
         first_kernel,
         [VM] * 4,
-        [(VM, chunks), (VM, (2, 8, LON))],
+        [(VM, chunks), (VM, (8, 8, LON)), (VM, (2, 8, LON))],
         scratch=[pltpu.VMEM((4,) + slab, f32)],
     )(tracer, thickness, wind_u, wind_v)
     factors = call(

time: 55.2 us -> 55.1 us (level)
  no operation moved by 1% of the time
where the time goes in v5:
time: 55.1 us; the launch traced here: 55 us
  blocking collectives  40 us (73%)
  Pallas kernels  6.96 us (13%)
  starting transfers between devices  4.49 us (8%)
  waiting for transfers between devices  2.71 us (5%)
  between operations  0.76 us (1%)
    all_to_all x2, blocking collectives, transposed(): return lax.all_to_all(block, 'lev', split_axis=0, concat_axis=0, tiled=True)  40 us
    ppermute x2, starting transfers between devices, local(): lax.ppermute(rows, ('lat', 'lev'), move)  4.49 us
    ppermute x2, waiting for transfers between devices, local(): lax.ppermute(rows, ('lat', 'lev'), move)  2.71 us
    pallas_call x1, Pallas kernels, local(): call(first_kernel, [VM] * 4, [(VM, chunks), (VM, (8, 8, LON)), (VM, (2, 8...  1.82 us
    pallas_call x1, Pallas kernels, local(): call(factor_kernel, [VM, VM], [(VM, (3, LEVELS, ROWS, LANES)), (VM, (3, L...  1.75 us
    pallas_call x1, Pallas kernels, local(): call(edge_kernel, [HB] * 4, [(VM, halo), (VM, halo)], scratch=[pltpu.VMEM...  1.42 us
  transfers between devices with their start and end apart: 2, of which 1 were waited for; matrix products, arithmetic and copies ran while one was open for 0% of the time, Pallas kernels for 6%

profile of v5, /device:TPU:70, one launch (start us, length us, event | category | flops | bytes accessed | tf_op | source)
XLA Modules:
  0.0 55.0 jit_solution(16065365964232616961)
XLA Ops:
  0.6 0.0 copy-start.3
  0.6 0.0 copy-start.2
  0.7 0.0 copy-start.1
  0.7 0.0 copy-start
  0.7 0.0 copy-start.5
  0.7 0.0 copy-start.4
  0.7 1.4 %shard_map.85 = (f32[5,2,2304]{2,1,0:T(2,128)S(1)}, f32[5,2,2304]{2,1,0:T(2,128)S(1)}) custom-call(f32[2,16,2304]{2,1,0:T(8,128)} %tracer.3, f32[2,16,2304]{2,1,0:T(8,128)} %thickness.3, f32[2,16,2304]{2,1,0:T(8,128)} %wind_u.3, f32[2,16,2304]{2,1,0:T(8,128)} %wind_v.3), custom_call_target="tpu_custom_call" | custom-call | flops 1000000 | bytes 3000000 | tf_op jit(solution)/shard_map/pallas_call | solution.py:374
  2.1 4.5 %collective-permute-start = (f32[5,2,2304]{2,1,0:T(2,128)S(1)}, f32[5,2,2304]{2,1,0:T(2,128)S(1)}, u32[]{:S(2)}, u32[]{:S(2)}) collective-permute-start(f32[5,2,2304]{2,1,0:T(2,128)S(1)} %get-tuple-element.13), channel_id=1, source_target_pairs={{0,1},{1,0},{2,3},{3,2},{4,5},{5,4},{6,7},{7,6},{8,9},{9,8},{10,11... | collective-permute-start | bytes 276488 | tf_op jit(solution)/shard_map/ppermute | solution.py:393
  6.6 0.0 collective-permute-start.1
  6.6 0.0 copy-done.3
  6.6 0.0 copy-done.2
  6.6 0.0 copy-done.1
  6.6 0.0 copy-done
  6.6 1.8 %shard_map.86 = (f32[16,144,128]{2,1,0:T(8,128)S(1)}, f32[8,8,2304]{2,1,0:T(8,128)S(1)}, f32[2,8,2304]{2,1,0:T(8,128)S(1)}) custom-call(f32[2,16,2304]{2,1,0:T(8,128)S(1)} %copy-done, f32[2,16,2304]{2,1,0:T(8,128)S(1)} %copy-done.1, f32[2,16,2304]{2,1,0:T(8,128)S(1)} %copy-done.2, f32[2,16,2304]{2,1,0:T(8,128)S(1)} %copy-done.3), custom_call_target="tpu_custom_call" | custom-call | flops 1000000 | bytes 3000000 | tf_op jit(solution)/shard_map/pallas_call | solution.py:395
  8.5 0.0 copy-done.5
  8.5 0.0 copy-done.4
  8.5 1.8 %shard_map.87 = (f32[3,32,16,128]{3,2,1,0:T(8,128)S(1)}, f32[3,32,8,128]{3,2,1,0:T(8,128)S(1)}) custom-call(s32[32,16,144]{2,1,0:T(8,128)S(1)} %copy-done.4, f32[31,16,144]{2,1,0:T(8,128)S(1)} %copy-done.5), custom_call_target="tpu_custom_call" | custom-call | flops 1000000 | bytes 3000000 | tf_op jit(solution)/shard_map/pallas_call | solution.py:401
  10.2 2.7 %collective-permute-done.first_halo = f32[5,2,2304]{2,1,0:T(2,128)S(1)} collective-permute-done((f32[5,2,2304]{2,1,0:T(2,128)S(1)}, f32[5,2,2304]{2,1,0:T(2,128)S(1)}, u32[]{:S(2)}, u32[]{:S(2)}) %collective-permute-start) | collective-permute-done | bytes 92192 | tf_op jit(solution)/shard_map/ppermute | solution.py:393
  13.0 0.0 collective-permute-done.1.second_halo
  13.0 0.5 shard_map.88
  13.5 22.3 %all_to_all.10.received = f32[16,144,128]{2,1,0:T(8,128)S(1)} all-to-all(f32[16,144,128]{2,1,0:T(8,128)S(1)} %shard_map.88), channel_id=1, replica_groups=mesh['lat'=16,'lev'=16] {'lev'}, dimensions={0} | all-to-all | bytes 2359296 | tf_op jit(solution)/shard_map/all_to_all | solution.py:368
  35.8 0.4 shard_map.89
  36.2 17.7 %all_to_all.11.received = f32[16,112,128]{2,1,0:T(8,128)S(1)} all-to-all(f32[16,112,128]{2,1,0:T(8,128)S(1)} %shard_map.89), channel_id=1, replica_groups=mesh['lat'=16,'lev'=16] {'lev'}, dimensions={0} | all-to-all | bytes 1835008 | tf_op jit(solution)/shard_map/all_to_all | solution.py:368
  53.9 1.1 %shard_map.90 = (f32[2,16,2304]{2,1,0:T(8,128)}, f32[2,16,2304]{2,1,0:T(8,128)}, f32[2,16,2304]{2,1,0:T(8,128)}) custom-call(f32[16,112,128]{2,1,0:T(8,128)S(1)} %all_to_all.11.received), custom_call_target="tpu_custom_call" | custom-call | flops 1000000 | bytes 3000000 | tf_op jit(solution)/shard_map/pallas_call | solution.py:417
Async XLA Ops:
  0.6 6.0 %copy-start.3 = (f32[2,16,2304]{2,1,0:T(8,128)S(1)}, f32[2,16,2304]{2,1,0:T(8,128)}, u32[]{:S(2)}) copy-start(f32[2,16,2304]{2,1,0:T(8,128)} %wind_v.3) | copy-start | bytes 884740
  0.6 6.0 %copy-start.2 = (f32[2,16,2304]{2,1,0:T(8,128)S(1)}, f32[2,16,2304]{2,1,0:T(8,128)}, u32[]{:S(2)}) copy-start(f32[2,16,2304]{2,1,0:T(8,128)} %wind_u.3) | copy-start | bytes 884740
  0.7 6.0 %copy-start.1 = (f32[2,16,2304]{2,1,0:T(8,128)S(1)}, f32[2,16,2304]{2,1,0:T(8,128)}, u32[]{:S(2)}) copy-start(f32[2,16,2304]{2,1,0:T(8,128)} %thickness.3) | copy-start | bytes 884740
  0.7 6.0 %copy-start = (f32[2,16,2304]{2,1,0:T(8,128)S(1)}, f32[2,16,2304]{2,1,0:T(8,128)}, u32[]{:S(2)}) copy-start(f32[2,16,2304]{2,1,0:T(8,128)} %tracer.3) | copy-start | bytes 884740
  0.7 7.8 %copy-start.5 = (f32[31,16,144]{2,1,0:T(8,128)S(1)}, f32[31,16,144]{2,1,0:T(8,128)}, u32[]{:S(2)}) copy-start(f32[31,16,144]{2,1,0:T(8,128)} %coupling.1) | copy-start | bytes 857092
  0.7 7.8 %copy-start.4 = (s32[32,16,144]{2,1,0:T(8,128)S(1)}, s32[32,16,144]{2,1,0:T(8,128)}, u32[]{:S(2)}) copy-start(s32[32,16,144]{2,1,0:T(8,128)} %offsets.1) | copy-start | bytes 884740
  2.1 10.8 %collective-permute-start = (f32[5,2,2304]{2,1,0:T(2,128)S(1)}, f32[5,2,2304]{2,1,0:T(2,128)S(1)}, u32[]{:S(2)}, u32[]{:S(2)}) collective-permute-start(f32[5,2,2304]{2,1,0:T(2,128)S(1)} %get-tuple-element.13), channel_id=1, source_target_pairs={{0,1},{1,0},{2,3},{3,2},{4,5},{5,4},{6,7},{7,6},{8,9},{9,8},{10,11... | collective-permute-start | bytes 276488 | tf_op jit(solution)/shard_map/ppermute | solution.py:393
  6.6 6.4 %collective-permute-start.1 = (f32[5,2,2304]{2,1,0:T(2,128)S(1)}, f32[5,2,2304]{2,1,0:T(2,128)S(1)}, u32[]{:S(2)}, u32[]{:S(2)}) collective-permute-start(f32[5,2,2304]{2,1,0:T(2,128)S(1)} %get-tuple-element.14), channel_id=1, source_target_pairs={{0,16},{1,17},{2,18},{3,19},{4,20},{5,21},{6,22},{7,23},{8,24},{9,... | collective-permute-start | bytes 276488 | tf_op jit(solution)/shard_map/ppermute | solution.py:393

commit v6 on v5

--- a/solution.py
+++ b/solution.py
@@ -50,24 +50,19 @@
 def edge_kernel(tracer, thickness, wind_u, wind_v, to_first, to_second, fetched, sems):
     copies = [
         pltpu.make_async_copy(
-            ref.at[:, pl.ds(14 * end, 2), :],
-            fetched.at[slot, :, pl.ds(2 * end, 2), :],
-            sems.at[2 * slot + end],
+            ref.at[level, pl.ds(14 * end, 2), :],
+            fetched.at[slot, pl.ds(6 - 4 * level if end else 4 * level, 2), :],
+            sems.at[4 * slot + 2 * level + end],
         )
         for slot, ref in enumerate((tracer, thickness, wind_u, wind_v))
+        for level in range(2)
         for end in range(2)
     ]
     for copy in copies:
         copy.start()
     for copy in copies:
         copy.wait()
-    tracer, layer, u, v = [
-        jnp.concatenate(
-            [fetched[slot, 0, 0:2], fetched[slot, 1, 2:4], fetched[slot, 1, 0:2], fetched[slot, 0, 2:4]],
-            axis=0,
-        )
-        for slot in range(4)
-    ]
+    tracer, layer, u, v = [fetched[slot] for slot in range(4)]
     mass = tracer * layer
     east = courant(east_roll(u) + u)
     north = courant(v + pltpu.roll(v, 7, 0))
@@ -375,7 +370,7 @@
         edge_kernel,
         [HB] * 4,
         [(VM, halo), (VM, halo)],
-        scratch=[pltpu.VMEM((4, 2, 4, LON), f32), pltpu.SemaphoreType.DMA((8,))],
+        scratch=[pltpu.VMEM((4, 8, LON), f32), pltpu.SemaphoreType.DMA((16,))],
     )(*fields)
     lev_count = lax.axis_size("lev")
     moves = []

time: 55.1 us -> 55.1 us (level)
  transfers between devices with their start and end apart: 2 -> 2, of which waited for: 1 -> 1; matrix products, arithmetic and copies ran while one was open for 0% -> 0% of each run, Pallas kernels for 6% -> 7%
where the time goes in v6:
time: 55.1 us; the launch traced here: 54.9 us
  blocking collectives  40 us (73%)
  Pallas kernels  6.93 us (13%)
  starting transfers between devices  4.49 us (8%)
  waiting for transfers between devices  2.71 us (5%)
  between operations  0.76 us (1%)
    all_to_all x2, blocking collectives, transposed(): return lax.all_to_all(block, 'lev', split_axis=0, concat_axis=0, tiled=True)  40 us
    ppermute x2, starting transfers between devices, local(): lax.ppermute(rows, ('lat', 'lev'), move)  4.49 us
    ppermute x2, waiting for transfers between devices, local(): lax.ppermute(rows, ('lat', 'lev'), move)  2.71 us
    pallas_call x1, Pallas kernels, local(): call(first_kernel, [VM] * 4, [(VM, chunks), (VM, (8, 8, LON)), (VM, (2, 8...  1.82 us
    pallas_call x1, Pallas kernels, local(): call(factor_kernel, [VM, VM], [(VM, (3, LEVELS, ROWS, LANES)), (VM, (3, L...  1.75 us
    pallas_call x1, Pallas kernels, local(): call(edge_kernel, [HB] * 4, [(VM, halo), (VM, halo)], scratch=[pltpu.VMEM...  1.4 us
  transfers between devices with their start and end apart: 2, of which 1 were waited for; matrix products, arithmetic and copies ran while one was open for 0% of the time, Pallas kernels for 7%

profile of v6, /device:TPU:70, one launch (start us, length us, event | category | flops | bytes accessed | tf_op | source)
XLA Modules:
  0.0 54.9 jit_solution(14568428427794845621)
XLA Ops:
  0.6 0.0 copy-start.3
  0.6 0.0 copy-start.2
  0.7 0.0 copy-start.1
  0.7 0.0 copy-start
  0.7 0.0 copy-start.5
  0.7 0.0 copy-start.4
  0.7 1.4 %shard_map.85 = (f32[5,2,2304]{2,1,0:T(2,128)S(1)}, f32[5,2,2304]{2,1,0:T(2,128)S(1)}) custom-call(f32[2,16,2304]{2,1,0:T(8,128)} %tracer.3, f32[2,16,2304]{2,1,0:T(8,128)} %thickness.3, f32[2,16,2304]{2,1,0:T(8,128)} %wind_u.3, f32[2,16,2304]{2,1,0:T(8,128)} %wind_v.3), custom_call_target="tpu_custom_call" | custom-call | flops 1000000 | bytes 3000000 | tf_op jit(solution)/shard_map/pallas_call | solution.py:369
  2.1 4.5 %collective-permute-start = (f32[5,2,2304]{2,1,0:T(2,128)S(1)}, f32[5,2,2304]{2,1,0:T(2,128)S(1)}, u32[]{:S(2)}, u32[]{:S(2)}) collective-permute-start(f32[5,2,2304]{2,1,0:T(2,128)S(1)} %get-tuple-element.13), channel_id=1, source_target_pairs={{0,1},{1,0},{2,3},{3,2},{4,5},{5,4},{6,7},{7,6},{8,9},{9,8},{10,11... | collective-permute-start | bytes 276488 | tf_op jit(solution)/shard_map/ppermute | solution.py:388
  6.6 0.0 collective-permute-start.1
  6.6 0.0 copy-done.3
  6.6 0.0 copy-done.2
  6.6 0.0 copy-done.1
  6.6 0.0 copy-done
  6.6 1.8 %shard_map.86 = (f32[16,144,128]{2,1,0:T(8,128)S(1)}, f32[8,8,2304]{2,1,0:T(8,128)S(1)}, f32[2,8,2304]{2,1,0:T(8,128)S(1)}) custom-call(f32[2,16,2304]{2,1,0:T(8,128)S(1)} %copy-done, f32[2,16,2304]{2,1,0:T(8,128)S(1)} %copy-done.1, f32[2,16,2304]{2,1,0:T(8,128)S(1)} %copy-done.2, f32[2,16,2304]{2,1,0:T(8,128)S(1)} %copy-done.3), custom_call_target="tpu_custom_call" | custom-call | flops 1000000 | bytes 3000000 | tf_op jit(solution)/shard_map/pallas_call | solution.py:390
  8.4 0.0 copy-done.5
  8.4 0.0 copy-done.4
  8.5 1.8 %shard_map.87 = (f32[3,32,16,128]{3,2,1,0:T(8,128)S(1)}, f32[3,32,8,128]{3,2,1,0:T(8,128)S(1)}) custom-call(s32[32,16,144]{2,1,0:T(8,128)S(1)} %copy-done.4, f32[31,16,144]{2,1,0:T(8,128)S(1)} %copy-done.5), custom_call_target="tpu_custom_call" | custom-call | flops 1000000 | bytes 3000000 | tf_op jit(solution)/shard_map/pallas_call | solution.py:396
  10.2 2.7 %collective-permute-done.first_halo = f32[5,2,2304]{2,1,0:T(2,128)S(1)} collective-permute-done((f32[5,2,2304]{2,1,0:T(2,128)S(1)}, f32[5,2,2304]{2,1,0:T(2,128)S(1)}, u32[]{:S(2)}, u32[]{:S(2)}) %collective-permute-start) | collective-permute-done | bytes 92192 | tf_op jit(solution)/shard_map/ppermute | solution.py:388
  12.9 0.0 collective-permute-done.1.second_halo
  12.9 0.5 shard_map.88
  13.5 22.3 %all_to_all.10.received = f32[16,144,128]{2,1,0:T(8,128)S(1)} all-to-all(f32[16,144,128]{2,1,0:T(8,128)S(1)} %shard_map.88), channel_id=1, replica_groups=mesh['lat'=16,'lev'=16] {'lev'}, dimensions={0} | all-to-all | bytes 2359296 | tf_op jit(solution)/shard_map/all_to_all | solution.py:363
  35.8 0.4 shard_map.89
  36.2 17.7 %all_to_all.11.received = f32[16,112,128]{2,1,0:T(8,128)S(1)} all-to-all(f32[16,112,128]{2,1,0:T(8,128)S(1)} %shard_map.89), channel_id=1, replica_groups=mesh['lat'=16,'lev'=16] {'lev'}, dimensions={0} | all-to-all | bytes 1835008 | tf_op jit(solution)/shard_map/all_to_all | solution.py:363
  53.9 1.1 %shard_map.90 = (f32[2,16,2304]{2,1,0:T(8,128)}, f32[2,16,2304]{2,1,0:T(8,128)}, f32[2,16,2304]{2,1,0:T(8,128)}) custom-call(f32[16,112,128]{2,1,0:T(8,128)S(1)} %all_to_all.11.received), custom_call_target="tpu_custom_call" | custom-call | flops 1000000 | bytes 3000000 | tf_op jit(solution)/shard_map/pallas_call | solution.py:412
Async XLA Ops:
  0.6 6.0 %copy-start.3 = (f32[2,16,2304]{2,1,0:T(8,128)S(1)}, f32[2,16,2304]{2,1,0:T(8,128)}, u32[]{:S(2)}) copy-start(f32[2,16,2304]{2,1,0:T(8,128)} %wind_v.3) | copy-start | bytes 884740
  0.6 5.9 %copy-start.2 = (f32[2,16,2304]{2,1,0:T(8,128)S(1)}, f32[2,16,2304]{2,1,0:T(8,128)}, u32[]{:S(2)}) copy-start(f32[2,16,2304]{2,1,0:T(8,128)} %wind_u.3) | copy-start | bytes 884740
  0.7 5.9 %copy-start.1 = (f32[2,16,2304]{2,1,0:T(8,128)S(1)}, f32[2,16,2304]{2,1,0:T(8,128)}, u32[]{:S(2)}) copy-start(f32[2,16,2304]{2,1,0:T(8,128)} %thickness.3) | copy-start | bytes 884740
  0.7 5.9 %copy-start = (f32[2,16,2304]{2,1,0:T(8,128)S(1)}, f32[2,16,2304]{2,1,0:T(8,128)}, u32[]{:S(2)}) copy-start(f32[2,16,2304]{2,1,0:T(8,128)} %tracer.3) | copy-start | bytes 884740
  0.7 7.8 %copy-start.5 = (f32[31,16,144]{2,1,0:T(8,128)S(1)}, f32[31,16,144]{2,1,0:T(8,128)}, u32[]{:S(2)}) copy-start(f32[31,16,144]{2,1,0:T(8,128)} %coupling.1) | copy-start | bytes 857092
  0.7 7.8 %copy-start.4 = (s32[32,16,144]{2,1,0:T(8,128)S(1)}, s32[32,16,144]{2,1,0:T(8,128)}, u32[]{:S(2)}) copy-start(s32[32,16,144]{2,1,0:T(8,128)} %offsets.1) | copy-start | bytes 884740
  2.1 10.8 %collective-permute-start = (f32[5,2,2304]{2,1,0:T(2,128)S(1)}, f32[5,2,2304]{2,1,0:T(2,128)S(1)}, u32[]{:S(2)}, u32[]{:S(2)}) collective-permute-start(f32[5,2,2304]{2,1,0:T(2,128)S(1)} %get-tuple-element.13), channel_id=1, source_target_pairs={{0,1},{1,0},{2,3},{3,2},{4,5},{5,4},{6,7},{7,6},{8,9},{9,8},{10,11... | collective-permute-start | bytes 276488 | tf_op jit(solution)/shard_map/ppermute | solution.py:388
  6.6 6.4 %collective-permute-start.1 = (f32[5,2,2304]{2,1,0:T(2,128)S(1)}, f32[5,2,2304]{2,1,0:T(2,128)S(1)}, u32[]{:S(2)}, u32[]{:S(2)}) collective-permute-start(f32[5,2,2304]{2,1,0:T(2,128)S(1)} %get-tuple-element.14), channel_id=1, source_target_pairs={{0,16},{1,17},{2,18},{3,19},{4,20},{5,21},{6,22},{7,23},{8,24},{9,... | collective-permute-start | bytes 276488 | tf_op jit(solution)/shard_map/ppermute | solution.py:388

commit v7 on v6

--- a/solution.py
+++ b/solution.py
@@ -330,11 +330,9 @@
                     old = jnp.where(lane >= place, rest, old) if place > 0 else rest
                     value = jnp.where(lane >= shift, value, old) if fresh else old
                 whole[field, level, :, tile * LANES : (tile + 1) * LANES] = value
-            copy = pltpu.make_async_copy(
-                whole.at[field, level], out.at[level], sems.at[2 * field + level]
-            )
-            copy.start()
-            copies.append(copy)
+        copy = pltpu.make_async_copy(whole.at[field], out, sems.at[field])
+        copy.start()
+        copies.append(copy)
     for copy in copies:
         copy.wait()
 
@@ -413,7 +411,7 @@
             unpack_kernel,
             [VM],
             [(ANY, slab)] * 3,
-            scratch=[pltpu.VMEM((3,) + slab, f32), pltpu.SemaphoreType.DMA((6,))],
+            scratch=[pltpu.VMEM((3,) + slab, f32), pltpu.SemaphoreType.DMA((3,))],
         )(returned)
     )
 

time: 55.1 us -> 55.1 us (level)
  no operation moved by 1% of the time
where the time goes in v7:
time: 55.1 us; the launch traced here: 54.9 us
  blocking collectives  40 us (73%)
  Pallas kernels  6.93 us (13%)
  starting transfers between devices  4.49 us (8%)
  waiting for transfers between devices  2.71 us (5%)
  between operations  0.76 us (1%)
    all_to_all x2, blocking collectives, transposed(): return lax.all_to_all(block, 'lev', split_axis=0, concat_axis=0, tiled=True)  40 us
    ppermute x2, starting transfers between devices, local(): lax.ppermute(rows, ('lat', 'lev'), move)  4.49 us
    ppermute x2, waiting for transfers between devices, local(): lax.ppermute(rows, ('lat', 'lev'), move)  2.71 us
    pallas_call x1, Pallas kernels, local(): call(first_kernel, [VM] * 4, [(VM, chunks), (VM, (8, 8, LON)), (VM, (2, 8...  1.82 us
    pallas_call x1, Pallas kernels, local(): call(factor_kernel, [VM, VM], [(VM, (3, LEVELS, ROWS, LANES)), (VM, (3, L...  1.75 us
    pallas_call x1, Pallas kernels, local(): call(edge_kernel, [HB] * 4, [(VM, halo), (VM, halo)], scratch=[pltpu.VMEM...  1.4 us
  transfers between devices with their start and end apart: 2, of which 1 were waited for; matrix products, arithmetic and copies ran while one was open for 0% of the time, Pallas kernels for 7%

profile of v7, /device:TPU:70, one launch (start us, length us, event | category | flops | bytes accessed | tf_op | source)
XLA Modules:
  0.0 54.9 jit_solution(7832094897467691315)
XLA Ops:
  0.6 0.0 copy-start.3
  0.6 0.0 copy-start.2
  0.7 0.0 copy-start.1
  0.7 0.0 copy-start
  0.7 0.0 copy-start.5
  0.7 0.0 copy-start.4
  0.7 1.4 %shard_map.85 = (f32[5,2,2304]{2,1,0:T(2,128)S(1)}, f32[5,2,2304]{2,1,0:T(2,128)S(1)}) custom-call(f32[2,16,2304]{2,1,0:T(8,128)} %tracer.3, f32[2,16,2304]{2,1,0:T(8,128)} %thickness.3, f32[2,16,2304]{2,1,0:T(8,128)} %wind_u.3, f32[2,16,2304]{2,1,0:T(8,128)} %wind_v.3), custom_call_target="tpu_custom_call" | custom-call | flops 1000000 | bytes 3000000 | tf_op jit(solution)/shard_map/pallas_call | solution.py:367
  2.1 4.5 %collective-permute-start = (f32[5,2,2304]{2,1,0:T(2,128)S(1)}, f32[5,2,2304]{2,1,0:T(2,128)S(1)}, u32[]{:S(2)}, u32[]{:S(2)}) collective-permute-start(f32[5,2,2304]{2,1,0:T(2,128)S(1)} %get-tuple-element.13), channel_id=1, source_target_pairs={{0,1},{1,0},{2,3},{3,2},{4,5},{5,4},{6,7},{7,6},{8,9},{9,8},{10,11... | collective-permute-start | bytes 276488 | tf_op jit(solution)/shard_map/ppermute | solution.py:386
  6.6 0.0 collective-permute-start.1
  6.6 0.0 copy-done.3
  6.6 0.0 copy-done.2
  6.6 0.0 copy-done.1
  6.6 0.0 copy-done
  6.6 1.8 %shard_map.86 = (f32[16,144,128]{2,1,0:T(8,128)S(1)}, f32[8,8,2304]{2,1,0:T(8,128)S(1)}, f32[2,8,2304]{2,1,0:T(8,128)S(1)}) custom-call(f32[2,16,2304]{2,1,0:T(8,128)S(1)} %copy-done, f32[2,16,2304]{2,1,0:T(8,128)S(1)} %copy-done.1, f32[2,16,2304]{2,1,0:T(8,128)S(1)} %copy-done.2, f32[2,16,2304]{2,1,0:T(8,128)S(1)} %copy-done.3), custom_call_target="tpu_custom_call" | custom-call | flops 1000000 | bytes 3000000 | tf_op jit(solution)/shard_map/pallas_call | solution.py:388
  8.4 0.0 copy-done.5
  8.4 0.0 copy-done.4
  8.5 1.8 %shard_map.87 = (f32[3,32,16,128]{3,2,1,0:T(8,128)S(1)}, f32[3,32,8,128]{3,2,1,0:T(8,128)S(1)}) custom-call(s32[32,16,144]{2,1,0:T(8,128)S(1)} %copy-done.4, f32[31,16,144]{2,1,0:T(8,128)S(1)} %copy-done.5), custom_call_target="tpu_custom_call" | custom-call | flops 1000000 | bytes 3000000 | tf_op jit(solution)/shard_map/pallas_call | solution.py:394
  10.2 2.7 %collective-permute-done.first_halo = f32[5,2,2304]{2,1,0:T(2,128)S(1)} collective-permute-done((f32[5,2,2304]{2,1,0:T(2,128)S(1)}, f32[5,2,2304]{2,1,0:T(2,128)S(1)}, u32[]{:S(2)}, u32[]{:S(2)}) %collective-permute-start) | collective-permute-done | bytes 92192 | tf_op jit(solution)/shard_map/ppermute | solution.py:386
  12.9 0.0 collective-permute-done.1.second_halo
  12.9 0.5 shard_map.88
  13.5 22.3 %all_to_all.10.received = f32[16,144,128]{2,1,0:T(8,128)S(1)} all-to-all(f32[16,144,128]{2,1,0:T(8,128)S(1)} %shard_map.88), channel_id=1, replica_groups=mesh['lat'=16,'lev'=16] {'lev'}, dimensions={0} | all-to-all | bytes 2359296 | tf_op jit(solution)/shard_map/all_to_all | solution.py:361
  35.8 0.4 shard_map.89
  36.2 17.7 %all_to_all.11.received = f32[16,112,128]{2,1,0:T(8,128)S(1)} all-to-all(f32[16,112,128]{2,1,0:T(8,128)S(1)} %shard_map.89), channel_id=1, replica_groups=mesh['lat'=16,'lev'=16] {'lev'}, dimensions={0} | all-to-all | bytes 1835008 | tf_op jit(solution)/shard_map/all_to_all | solution.py:361
  53.9 1.1 %shard_map.90 = (f32[2,16,2304]{2,1,0:T(8,128)}, f32[2,16,2304]{2,1,0:T(8,128)}, f32[2,16,2304]{2,1,0:T(8,128)}) custom-call(f32[16,112,128]{2,1,0:T(8,128)S(1)} %all_to_all.11.received), custom_call_target="tpu_custom_call" | custom-call | flops 1000000 | bytes 3000000 | tf_op jit(solution)/shard_map/pallas_call | solution.py:410
Async XLA Ops:
  0.6 6.0 %copy-start.3 = (f32[2,16,2304]{2,1,0:T(8,128)S(1)}, f32[2,16,2304]{2,1,0:T(8,128)}, u32[]{:S(2)}) copy-start(f32[2,16,2304]{2,1,0:T(8,128)} %wind_v.3) | copy-start | bytes 884740
  0.6 5.9 %copy-start.2 = (f32[2,16,2304]{2,1,0:T(8,128)S(1)}, f32[2,16,2304]{2,1,0:T(8,128)}, u32[]{:S(2)}) copy-start(f32[2,16,2304]{2,1,0:T(8,128)} %wind_u.3) | copy-start | bytes 884740
  0.7 5.9 %copy-start.1 = (f32[2,16,2304]{2,1,0:T(8,128)S(1)}, f32[2,16,2304]{2,1,0:T(8,128)}, u32[]{:S(2)}) copy-start(f32[2,16,2304]{2,1,0:T(8,128)} %thickness.3) | copy-start | bytes 884740
  0.7 5.9 %copy-start = (f32[2,16,2304]{2,1,0:T(8,128)S(1)}, f32[2,16,2304]{2,1,0:T(8,128)}, u32[]{:S(2)}) copy-start(f32[2,16,2304]{2,1,0:T(8,128)} %tracer.3) | copy-start | bytes 884740
  0.7 7.8 %copy-start.5 = (f32[31,16,144]{2,1,0:T(8,128)S(1)}, f32[31,16,144]{2,1,0:T(8,128)}, u32[]{:S(2)}) copy-start(f32[31,16,144]{2,1,0:T(8,128)} %coupling.1) | copy-start | bytes 857092
  0.7 7.8 %copy-start.4 = (s32[32,16,144]{2,1,0:T(8,128)S(1)}, s32[32,16,144]{2,1,0:T(8,128)}, u32[]{:S(2)}) copy-start(s32[32,16,144]{2,1,0:T(8,128)} %offsets.1) | copy-start | bytes 884740
  2.1 10.8 %collective-permute-start = (f32[5,2,2304]{2,1,0:T(2,128)S(1)}, f32[5,2,2304]{2,1,0:T(2,128)S(1)}, u32[]{:S(2)}, u32[]{:S(2)}) collective-permute-start(f32[5,2,2304]{2,1,0:T(2,128)S(1)} %get-tuple-element.13), channel_id=1, source_target_pairs={{0,1},{1,0},{2,3},{3,2},{4,5},{5,4},{6,7},{7,6},{8,9},{9,8},{10,11... | collective-permute-start | bytes 276488 | tf_op jit(solution)/shard_map/ppermute | solution.py:386
  6.6 6.4 %collective-permute-start.1 = (f32[5,2,2304]{2,1,0:T(2,128)S(1)}, f32[5,2,2304]{2,1,0:T(2,128)S(1)}, u32[]{:S(2)}, u32[]{:S(2)}) collective-permute-start(f32[5,2,2304]{2,1,0:T(2,128)S(1)} %get-tuple-element.14), channel_id=1, source_target_pairs={{0,16},{1,17},{2,18},{3,19},{4,20},{5,21},{6,22},{7,23},{8,24},{9,... | collective-permute-start | bytes 276488 | tf_op jit(solution)/shard_map/ppermute | solution.py:386
